TPU v7x, 32 devices: a whole 2x2x4 slice. The times are simulated.
32 devices in a mesh: group: 2 (over y), chan: 4 (over x, core), tm: 4 (over z).
Axes of the slice: x: 2, y: 2, z: 4, core: 2. Of those that a mesh axis runs over, the one named last changes fastest.
Arguments:
- voltages: bfloat16 [2, 32, 1024, 1024], P(None, ('group', 'tm'), 'chan'), parts along dimension 1, may hold values from -6 to 6
- feed_position: int32 [1024, 2], replicated, may hold values from 0 to 63
- beam_steering: int32 [256, 2], P('group'), parts along dimension 0, may hold values from 0 to 63
- synthesis_taps: float32 [4, 1024], replicated, may hold values from 0.2 to 1
Outputs:
- synthesized: bfloat16 [2, 128, 32, 1024], P(None, 'chan', ('group', 'tm')), parts along dimension 2
There are 2 independent parts, one for each index of `group`. A program takes and returns all parts, laid end to end along the dimension named above; an argument that names none is the same for every part. Nothing has to cross between parts.
All inputs are finite; a program needn't handle non-finite values.
Results may differ from a plain program's by a relative error of at most 0.0085.
Values may be sent and summed in bfloat16 or wider, within the bound.
A program may use at most 64 MiB of HBM per device.

v0:
```python
import math

import jax
import jax.numpy as jnp
from jax import lax
from jax.sharding import PartitionSpec as P

F = 1024
C = 1024
BEAMS = 128
TAPS = 4
PHASES = 4096


def passed_along(value, axis, steps):
    count = lax.axis_size(axis)
    initial, last = (max(0, -steps), min(count, count - steps))
    return lax.ppermute(value, axis, [(source, source + steps) for source in range(initial, last)])


def compute_delays(feed_position, beam_steering):
    first = feed_position[:, 0:1] * beam_steering[:, 0][None, :]
    second = feed_position[:, 1:2] * beam_steering[:, 1][None, :]
    return (first + second) % PHASES


def make_weights(delays, channel_ids):
    phases = channel_ids[:, None, None] * delays[None, :, :] % PHASES
    angles = phases.astype(jnp.float32) * (2.0 * math.pi / PHASES)
    return jnp.concatenate([jnp.cos(angles), jnp.sin(angles)], axis=-1).astype(jnp.bfloat16)


def combine(product):
    half = product.shape[-1] // 2
    real_part = product[0, ..., :half] - product[1, ..., half:]
    imag_part = product[0, ..., half:] + product[1, ..., :half]
    return (jnp.stack([real_part, imag_part]) * (1.0 / math.sqrt(F))).astype(jnp.bfloat16)


def make_basis():
    rows = lax.iota(jnp.int32, C)
    products = rows[:, None] * rows[None, :] % C
    angles = products.astype(jnp.float32) * (2.0 * math.pi / C)
    cosine = jnp.cos(angles)
    sine = jnp.sin(angles)
    upper = jnp.concatenate([cosine, sine], axis=1)
    lower = jnp.concatenate([-sine, cosine], axis=1)
    return jnp.stack([upper, lower]).astype(jnp.bfloat16)


def beamform(turned, delays, channel_ids):
    chan_count = turned.shape[3]
    width = math.gcd(chan_count, 8)
    count = chan_count // width

    def one_block(block_index, result):
        offset = block_index * width
        slab = lax.dynamic_slice_in_dim(turned, offset, width, 3)
        block_ids = lax.dynamic_slice_in_dim(channel_ids, offset, width, 0)
        weights = make_weights(delays, block_ids)
        product = jnp.einsum("stfc,cfk->stck", slab, weights, preferred_element_type=jnp.float32)
        return lax.dynamic_update_slice_in_dim(result, combine(product), offset, 2)

    initial = jnp.zeros((2, turned.shape[1], chan_count, BEAMS), jnp.bfloat16)
    return lax.fori_loop(0, count, one_block, initial)


def synthesize(beamed, basis):
    frames = jnp.einsum("stcb,scn->tbn", beamed, basis, preferred_element_type=jnp.float32)
    return (frames * (1.0 / math.sqrt(C))).astype(jnp.bfloat16)


def apply_taps(extended, synthesis_taps):
    frame_count = extended.shape[0] - (TAPS - 1)
    widened = extended.astype(jnp.float32)
    doubled = jnp.concatenate([synthesis_taps, synthesis_taps], axis=1)
    total = jnp.zeros((frame_count,) + extended.shape[1:], jnp.float32)
    for tap_index in range(TAPS):
        begin = TAPS - 1 - tap_index
        total = total + doubled[tap_index][None, None, :] * widened[begin : begin + frame_count]
    output = total.astype(jnp.bfloat16).reshape(frame_count, extended.shape[1], 2, C)
    return jnp.transpose(output, (2, 1, 0, 3))


def on_device(voltages, feed_position, beam_steering, synthesis_taps):
    devices_chan = lax.axis_size("chan")
    chan_count = C // devices_chan
    chan_start = lax.axis_index("chan") * chan_count
    delays = compute_delays(feed_position, beam_steering)
    turned = lax.all_to_all(voltages, "chan", split_axis=3, concat_axis=2, tiled=True)
    channel_ids = chan_start + lax.iota(jnp.int32, chan_count)
    beamed = beamform(turned, delays, channel_ids)
    regrouped = lax.all_to_all(beamed, "chan", split_axis=3, concat_axis=2, tiled=True)
    basis = make_basis()
    frames = synthesize(regrouped, basis)
    carried = passed_along(frames[frames.shape[0] - (TAPS - 1) :], "tm", 1)
    extended = jnp.concatenate([carried, frames], axis=0)
    return apply_taps(extended, synthesis_taps)


def solution(mesh):
    return jax.shard_map(
        on_device,
        mesh=mesh,
        in_specs=(P(None, ("group", "tm"), "chan", None), P(), P("group", None), P()),
        out_specs=P(None, "chan", ("group", "tm"), None),
        check_vma=False,
    )
```

profile of v0, /device:TPU:0, one launch (start us, length us, event | category | flops | bytes accessed | tf_op | source)
XLA Modules:
  0.0 706.9 jit_solution(326471014404015039)
XLA Ops:
  28.7 17.8 %negate_convert_fusion = (bf16[1024,1024]{1,0:T(8,128)(2,1)}, bf16[1024,1024]{1,0:T(8,128)(2,1)}) fusion(), kind=kLoop, calls=%fused_computation.36 | loop fusion | flops 17825792 | bytes 4194304 | tf_op jit(solution)/shard_map/convert.5
  68.4 605.1 %while.16 = (s32[]{:T(128)}, bf16[2,4,256,128]{3,1,0,2:T(4,128)(2,1)S(1)}, s32[256]{0:T(256)S(1)}, bf16[2,4,1024,256]{2,1,0,3:T(4,128)(2,1)}, s32[128]{0:T(128)S...) while((s32[]{:T(128)}, ...), condition=%wide.region_1.2_spmd.clone, body=%wide.region_0.1_spmd.clone.sunk | while | flops 60588036 | bytes 9790735 | solution.py:65
  68.9 16.8 %cosine_convert_fusion.3 = (bf16[8,1024,128]{2,1,0:T(8,128)(2,1)S(1)}, bf16[8,1024,128]{2,1,0:T(8,128)(2,1)S(1)}) fusion(s32[1024,128]{1,0:T(8,128)S(1)} %add_select_fusion.4, s32[8]{0:T(128)S(1)} %dynamic_slice.27), kind=kLoop, calls=%fused_computation.11.clone.1 | loop fusion | flops 16777216 | bytes 4718624 | tf_op jit(solution)/shard_map/convert
  87.8 16.8 %cosine_convert_fusion.3 = (bf16[8,1024,128]{2,1,0:T(8,128)(2,1)S(1)}, bf16[8,1024,128]{2,1,0:T(8,128)(2,1)S(1)}) fusion(s32[1024,128]{1,0:T(8,128)S(1)} %add_select_fusion.4, s32[8]{0:T(128)S(1)} %dynamic_slice.27), kind=kLoop, calls=%fused_computation.11.clone.1 | loop fusion | flops 16777216 | bytes 4718624 | tf_op jit(solution)/shard_map/convert
  106.7 16.8 %cosine_convert_fusion.3 = (bf16[8,1024,128]{2,1,0:T(8,128)(2,1)S(1)}, bf16[8,1024,128]{2,1,0:T(8,128)(2,1)S(1)}) fusion(s32[1024,128]{1,0:T(8,128)S(1)} %add_select_fusion.4, s32[8]{0:T(128)S(1)} %dynamic_slice.27), kind=kLoop, calls=%fused_computation.11.clone.1 | loop fusion | flops 16777216 | bytes 4718624 | tf_op jit(solution)/shard_map/convert
  125.6 16.8 %cosine_convert_fusion.3 = (bf16[8,1024,128]{2,1,0:T(8,128)(2,1)S(1)}, bf16[8,1024,128]{2,1,0:T(8,128)(2,1)S(1)}) fusion(s32[1024,128]{1,0:T(8,128)S(1)} %add_select_fusion.4, s32[8]{0:T(128)S(1)} %dynamic_slice.27), kind=kLoop, calls=%fused_computation.11.clone.1 | loop fusion | flops 16777216 | bytes 4718624 | tf_op jit(solution)/shard_map/convert
  144.5 16.8 %cosine_convert_fusion.3 = (bf16[8,1024,128]{2,1,0:T(8,128)(2,1)S(1)}, bf16[8,1024,128]{2,1,0:T(8,128)(2,1)S(1)}) fusion(s32[1024,128]{1,0:T(8,128)S(1)} %add_select_fusion.4, s32[8]{0:T(128)S(1)} %dynamic_slice.27), kind=kLoop, calls=%fused_computation.11.clone.1 | loop fusion | flops 16777216 | bytes 4718624 | tf_op jit(solution)/shard_map/convert
  163.4 16.8 %cosine_convert_fusion.3 = (bf16[8,1024,128]{2,1,0:T(8,128)(2,1)S(1)}, bf16[8,1024,128]{2,1,0:T(8,128)(2,1)S(1)}) fusion(s32[1024,128]{1,0:T(8,128)S(1)} %add_select_fusion.4, s32[8]{0:T(128)S(1)} %dynamic_slice.27), kind=kLoop, calls=%fused_computation.11.clone.1 | loop fusion | flops 16777216 | bytes 4718624 | tf_op jit(solution)/shard_map/convert
  182.3 16.8 %cosine_convert_fusion.3 = (bf16[8,1024,128]{2,1,0:T(8,128)(2,1)S(1)}, bf16[8,1024,128]{2,1,0:T(8,128)(2,1)S(1)}) fusion(s32[1024,128]{1,0:T(8,128)S(1)} %add_select_fusion.4, s32[8]{0:T(128)S(1)} %dynamic_slice.27), kind=kLoop, calls=%fused_computation.11.clone.1 | loop fusion | flops 16777216 | bytes 4718624 | tf_op jit(solution)/shard_map/convert
  201.2 16.8 %cosine_convert_fusion.3 = (bf16[8,1024,128]{2,1,0:T(8,128)(2,1)S(1)}, bf16[8,1024,128]{2,1,0:T(8,128)(2,1)S(1)}) fusion(s32[1024,128]{1,0:T(8,128)S(1)} %add_select_fusion.4, s32[8]{0:T(128)S(1)} %dynamic_slice.27), kind=kLoop, calls=%fused_computation.11.clone.1 | loop fusion | flops 16777216 | bytes 4718624 | tf_op jit(solution)/shard_map/convert
  220.2 16.8 %cosine_convert_fusion.3 = (bf16[8,1024,128]{2,1,0:T(8,128)(2,1)S(1)}, bf16[8,1024,128]{2,1,0:T(8,128)(2,1)S(1)}) fusion(s32[1024,128]{1,0:T(8,128)S(1)} %add_select_fusion.4, s32[8]{0:T(128)S(1)} %dynamic_slice.27), kind=kLoop, calls=%fused_computation.11.clone.1 | loop fusion | flops 16777216 | bytes 4718624 | tf_op jit(solution)/shard_map/convert
  239.1 16.8 %cosine_convert_fusion.3 = (bf16[8,1024,128]{2,1,0:T(8,128)(2,1)S(1)}, bf16[8,1024,128]{2,1,0:T(8,128)(2,1)S(1)}) fusion(s32[1024,128]{1,0:T(8,128)S(1)} %add_select_fusion.4, s32[8]{0:T(128)S(1)} %dynamic_slice.27), kind=kLoop, calls=%fused_computation.11.clone.1 | loop fusion | flops 16777216 | bytes 4718624 | tf_op jit(solution)/shard_map/convert
  258.0 16.8 %cosine_convert_fusion.3 = (bf16[8,1024,128]{2,1,0:T(8,128)(2,1)S(1)}, bf16[8,1024,128]{2,1,0:T(8,128)(2,1)S(1)}) fusion(s32[1024,128]{1,0:T(8,128)S(1)} %add_select_fusion.4, s32[8]{0:T(128)S(1)} %dynamic_slice.27), kind=kLoop, calls=%fused_computation.11.clone.1 | loop fusion | flops 16777216 | bytes 4718624 | tf_op jit(solution)/shard_map/convert
  276.9 16.8 %cosine_convert_fusion.3 = (bf16[8,1024,128]{2,1,0:T(8,128)(2,1)S(1)}, bf16[8,1024,128]{2,1,0:T(8,128)(2,1)S(1)}) fusion(s32[1024,128]{1,0:T(8,128)S(1)} %add_select_fusion.4, s32[8]{0:T(128)S(1)} %dynamic_slice.27), kind=kLoop, calls=%fused_computation.11.clone.1 | loop fusion | flops 16777216 | bytes 4718624 | tf_op jit(solution)/shard_map/convert
  295.8 16.8 %cosine_convert_fusion.3 = (bf16[8,1024,128]{2,1,0:T(8,128)(2,1)S(1)}, bf16[8,1024,128]{2,1,0:T(8,128)(2,1)S(1)}) fusion(s32[1024,128]{1,0:T(8,128)S(1)} %add_select_fusion.4, s32[8]{0:T(128)S(1)} %dynamic_slice.27), kind=kLoop, calls=%fused_computation.11.clone.1 | loop fusion | flops 16777216 | bytes 4718624 | tf_op jit(solution)/shard_map/convert
  314.7 16.8 %cosine_convert_fusion.3 = (bf16[8,1024,128]{2,1,0:T(8,128)(2,1)S(1)}, bf16[8,1024,128]{2,1,0:T(8,128)(2,1)S(1)}) fusion(s32[1024,128]{1,0:T(8,128)S(1)} %add_select_fusion.4, s32[8]{0:T(128)S(1)} %dynamic_slice.27), kind=kLoop, calls=%fused_computation.11.clone.1 | loop fusion | flops 16777216 | bytes 4718624 | tf_op jit(solution)/shard_map/convert
  333.6 16.8 %cosine_convert_fusion.3 = (bf16[8,1024,128]{2,1,0:T(8,128)(2,1)S(1)}, bf16[8,1024,128]{2,1,0:T(8,128)(2,1)S(1)}) fusion(s32[1024,128]{1,0:T(8,128)S(1)} %add_select_fusion.4, s32[8]{0:T(128)S(1)} %dynamic_slice.27), kind=kLoop, calls=%fused_computation.11.clone.1 | loop fusion | flops 16777216 | bytes 4718624 | tf_op jit(solution)/shard_map/convert
  352.5 16.8 %cosine_convert_fusion.3 = (bf16[8,1024,128]{2,1,0:T(8,128)(2,1)S(1)}, bf16[8,1024,128]{2,1,0:T(8,128)(2,1)S(1)}) fusion(s32[1024,128]{1,0:T(8,128)S(1)} %add_select_fusion.4, s32[8]{0:T(128)S(1)} %dynamic_slice.27), kind=kLoop, calls=%fused_computation.11.clone.1 | loop fusion | flops 16777216 | bytes 4718624 | tf_op jit(solution)/shard_map/convert
  371.4 16.8 %cosine_convert_fusion.3 = (bf16[8,1024,128]{2,1,0:T(8,128)(2,1)S(1)}, bf16[8,1024,128]{2,1,0:T(8,128)(2,1)S(1)}) fusion(s32[1024,128]{1,0:T(8,128)S(1)} %add_select_fusion.4, s32[8]{0:T(128)S(1)} %dynamic_slice.27), kind=kLoop, calls=%fused_computation.11.clone.1 | loop fusion | flops 16777216 | bytes 4718624 | tf_op jit(solution)/shard_map/convert
  390.3 16.8 %cosine_convert_fusion.3 = (bf16[8,1024,128]{2,1,0:T(8,128)(2,1)S(1)}, bf16[8,1024,128]{2,1,0:T(8,128)(2,1)S(1)}) fusion(s32[1024,128]{1,0:T(8,128)S(1)} %add_select_fusion.4, s32[8]{0:T(128)S(1)} %dynamic_slice.27), kind=kLoop, calls=%fused_computation.11.clone.1 | loop fusion | flops 16777216 | bytes 4718624 | tf_op jit(solution)/shard_map/convert
  409.3 16.8 %cosine_convert_fusion.3 = (bf16[8,1024,128]{2,1,0:T(8,128)(2,1)S(1)}, bf16[8,1024,128]{2,1,0:T(8,128)(2,1)S(1)}) fusion(s32[1024,128]{1,0:T(8,128)S(1)} %add_select_fusion.4, s32[8]{0:T(128)S(1)} %dynamic_slice.27), kind=kLoop, calls=%fused_computation.11.clone.1 | loop fusion | flops 16777216 | bytes 4718624 | tf_op jit(solution)/shard_map/convert
  428.2 16.8 %cosine_convert_fusion.3 = (bf16[8,1024,128]{2,1,0:T(8,128)(2,1)S(1)}, bf16[8,1024,128]{2,1,0:T(8,128)(2,1)S(1)}) fusion(s32[1024,128]{1,0:T(8,128)S(1)} %add_select_fusion.4, s32[8]{0:T(128)S(1)} %dynamic_slice.27), kind=kLoop, calls=%fused_computation.11.clone.1 | loop fusion | flops 16777216 | bytes 4718624 | tf_op jit(solution)/shard_map/convert
  447.1 16.8 %cosine_convert_fusion.3 = (bf16[8,1024,128]{2,1,0:T(8,128)(2,1)S(1)}, bf16[8,1024,128]{2,1,0:T(8,128)(2,1)S(1)}) fusion(s32[1024,128]{1,0:T(8,128)S(1)} %add_select_fusion.4, s32[8]{0:T(128)S(1)} %dynamic_slice.27), kind=kLoop, calls=%fused_computation.11.clone.1 | loop fusion | flops 16777216 | bytes 4718624 | tf_op jit(solution)/shard_map/convert
  466.0 16.8 %cosine_convert_fusion.3 = (bf16[8,1024,128]{2,1,0:T(8,128)(2,1)S(1)}, bf16[8,1024,128]{2,1,0:T(8,128)(2,1)S(1)}) fusion(s32[1024,128]{1,0:T(8,128)S(1)} %add_select_fusion.4, s32[8]{0:T(128)S(1)} %dynamic_slice.27), kind=kLoop, calls=%fused_computation.11.clone.1 | loop fusion | flops 16777216 | bytes 4718624 | tf_op jit(solution)/shard_map/convert
  484.9 16.8 %cosine_convert_fusion.3 = (bf16[8,1024,128]{2,1,0:T(8,128)(2,1)S(1)}, bf16[8,1024,128]{2,1,0:T(8,128)(2,1)S(1)}) fusion(s32[1024,128]{1,0:T(8,128)S(1)} %add_select_fusion.4, s32[8]{0:T(128)S(1)} %dynamic_slice.27), kind=kLoop, calls=%fused_computation.11.clone.1 | loop fusion | flops 16777216 | bytes 4718624 | tf_op jit(solution)/shard_map/convert
  503.8 16.8 %cosine_convert_fusion.3 = (bf16[8,1024,128]{2,1,0:T(8,128)(2,1)S(1)}, bf16[8,1024,128]{2,1,0:T(8,128)(2,1)S(1)}) fusion(s32[1024,128]{1,0:T(8,128)S(1)} %add_select_fusion.4, s32[8]{0:T(128)S(1)} %dynamic_slice.27), kind=kLoop, calls=%fused_computation.11.clone.1 | loop fusion | flops 16777216 | bytes 4718624 | tf_op jit(solution)/shard_map/convert
  522.7 16.8 %cosine_convert_fusion.3 = (bf16[8,1024,128]{2,1,0:T(8,128)(2,1)S(1)}, bf16[8,1024,128]{2,1,0:T(8,128)(2,1)S(1)}) fusion(s32[1024,128]{1,0:T(8,128)S(1)} %add_select_fusion.4, s32[8]{0:T(128)S(1)} %dynamic_slice.27), kind=kLoop, calls=%fused_computation.11.clone.1 | loop fusion | flops 16777216 | bytes 4718624 | tf_op jit(solution)/shard_map/convert
  541.6 16.8 %cosine_convert_fusion.3 = (bf16[8,1024,128]{2,1,0:T(8,128)(2,1)S(1)}, bf16[8,1024,128]{2,1,0:T(8,128)(2,1)S(1)}) fusion(s32[1024,128]{1,0:T(8,128)S(1)} %add_select_fusion.4, s32[8]{0:T(128)S(1)} %dynamic_slice.27), kind=kLoop, calls=%fused_computation.11.clone.1 | loop fusion | flops 16777216 | bytes 4718624 | tf_op jit(solution)/shard_map/convert
  560.5 16.8 %cosine_convert_fusion.3 = (bf16[8,1024,128]{2,1,0:T(8,128)(2,1)S(1)}, bf16[8,1024,128]{2,1,0:T(8,128)(2,1)S(1)}) fusion(s32[1024,128]{1,0:T(8,128)S(1)} %add_select_fusion.4, s32[8]{0:T(128)S(1)} %dynamic_slice.27), kind=kLoop, calls=%fused_computation.11.clone.1 | loop fusion | flops 16777216 | bytes 4718624 | tf_op jit(solution)/shard_map/convert
  579.4 16.8 %cosine_convert_fusion.3 = (bf16[8,1024,128]{2,1,0:T(8,128)(2,1)S(1)}, bf16[8,1024,128]{2,1,0:T(8,128)(2,1)S(1)}) fusion(s32[1024,128]{1,0:T(8,128)S(1)} %add_select_fusion.4, s32[8]{0:T(128)S(1)} %dynamic_slice.27), kind=kLoop, calls=%fused_computation.11.clone.1 | loop fusion | flops 16777216 | bytes 4718624 | tf_op jit(solution)/shard_map/convert
  598.4 16.8 %cosine_convert_fusion.3 = (bf16[8,1024,128]{2,1,0:T(8,128)(2,1)S(1)}, bf16[8,1024,128]{2,1,0:T(8,128)(2,1)S(1)}) fusion(s32[1024,128]{1,0:T(8,128)S(1)} %add_select_fusion.4, s32[8]{0:T(128)S(1)} %dynamic_slice.27), kind=kLoop, calls=%fused_computation.11.clone.1 | loop fusion | flops 16777216 | bytes 4718624 | tf_op jit(solution)/shard_map/convert
  617.3 16.8 %cosine_convert_fusion.3 = (bf16[8,1024,128]{2,1,0:T(8,128)(2,1)S(1)}, bf16[8,1024,128]{2,1,0:T(8,128)(2,1)S(1)}) fusion(s32[1024,128]{1,0:T(8,128)S(1)} %add_select_fusion.4, s32[8]{0:T(128)S(1)} %dynamic_slice.27), kind=kLoop, calls=%fused_computation.11.clone.1 | loop fusion | flops 16777216 | bytes 4718624 | tf_op jit(solution)/shard_map/convert
  (195 shorter events, 182.0 us)
Async XLA Ops:
  7.9 5.0 copy-start
  7.9 5.1 copy-start.2
  7.9 5.1 copy-start.1
  7.9 53.8 %all-to-all-start = ((bf16[2,4,256,1024]{2,1,0,3:T(4,128)(2,1)}), bf16[2,4,256,1024]{2,1,0,3:T(4,128)(2,1)}, u32[]{:S(2)}, u32[]{:S(2)}) async-start(bf16[2,4,256,1024]{2,1,0,3:T(4,128)(2,1)} %copy.12), calls=%async_computation | async-start | bytes 8388608 | tf_op jit(solution)/shard_map/all_to_all | solution.py:90
  674.9 12.3 %all-to-all-start.1 = ((bf16[2,4,256,128]{2,1,0,3:T(4,128)(2,1)}), bf16[2,4,256,128]{2,1,0,3:T(4,128)(2,1)S(1)}, u32[]{:S(2)}, u32[]{:S(2)}) async-start(bf16[2,4,256,128]{2,1,0,3:T(4,128)(2,1)} %copy.14), calls=%async_computation.1 | async-start | bytes 1048576 | tf_op jit(solution)/shard_map/all_to_all | solution.py:93
  692.4 12.5 %collective-permute-start = (bf16[3,32,2048]{2,1,0:T(8,128)(2,1)S(1)}, bf16[3,32,2048]{2,1,0:T(8,128)(2,1)S(1)}, u32[]{:S(2)}, u32[]{:S(2)}) collective-permute-start(bf16[3,32,2048]{2,1,0:T(8,128)(2,1)S(1)} %slice.101), channel_id=1, source_target_pairs={{0,1},{1,2},{2,3},{4,5},{5,6},{6,7},{8,9},{9,10},{10,11},{12,13},{... | collective-permute-start | bytes 1179656 | tf_op jit(solution)/shard_map/ppermute | solution.py:18
where the time goes:
time: 708 us; the launch traced here: 707 us
  other arithmetic  591 us (83%)
  matrix products  54.3 us (8%)
  waiting for transfers between devices  25.6 us (4%)
  local copies, waits for them, and re-layouts  20.9 us (3%)
  starting transfers between devices  13 us (2%)
    another operation x34, other arithmetic  573 us
    dot_general x32, matrix products, one_block(): jnp.einsum('stfc,cfk->stck', slab, weights, preferred_element_type=jnp.fl...  50 us
    all_to_all x1, waiting for transfers between devices, on_device(): lax.all_to_all(voltages, 'chan', split_axis=3, concat_axis=2, tiled=True)  15.2 us
  transfers between devices with their start and end apart: 3, of which 3 were waited for; matrix products, arithmetic and copies ran while one was open for 6% of the time, Pallas kernels for 0%

commit v1 on v0

v1 whole, which is shorter than its diff:
```python
import functools
import math

import jax
import jax.numpy as jnp
from jax import lax
from jax.experimental import pallas as pl
from jax.experimental.pallas import tpu as pltpu
from jax.sharding import PartitionSpec as P

PHASES = 4096
ROWS = 32
DEPTH = 256


def passed_along(value, axis, steps):
    count = lax.axis_size(axis)
    initial, last = (max(0, -steps), min(count, count - steps))
    return lax.ppermute(value, axis, [(source, source + steps) for source in range(initial, last)])


def compute_delays(feed_position, beam_steering):
    first = feed_position[:, 0:1] * beam_steering[:, 0][None, :]
    second = feed_position[:, 1:2] * beam_steering[:, 1][None, :]
    return (first + second) % PHASES


def turn(steps, period):
    angles = (steps % period).astype(jnp.float32) * (2.0 * math.pi / period)
    return jnp.stack([jnp.cos(angles), jnp.sin(angles)])


def times(ar, ai, br, bi):
    return ar * br - ai * bi, ar * bi + ai * br


def beam_kernel(scale, v_ref, first_ref, unit_ref, out_ref, low_ref, high_ref, stride_ref, rounded_ref):
    width, rows, feeds = v_ref.shape
    half = rows // 2
    beams = first_ref.shape[2]
    bf16 = jnp.bfloat16

    @pl.when(pl.program_id(0) == 0)
    def _():
        @pl.loop(0, feeds // ROWS)
        def _(block):
            here = pl.ds(pl.multiple_of(block * ROWS, ROWS), ROWS)
            ur, ui = unit_ref[0, here, :], unit_ref[1, here, :]
            ar, ai = jnp.ones_like(ur), jnp.zeros_like(ui)
            for j in range(width):
                low_ref[j, 0, here, :] = ar.astype(bf16)
                low_ref[j, 1, here, :] = ai.astype(bf16)
                ar, ai = times(ar, ai, ur, ui)
            stride_ref[0, here, :] = ar
            stride_ref[1, here, :] = ai
            fr, fi = first_ref[0, here, :], first_ref[1, here, :]
            high_ref[0, here, :] = fr
            high_ref[1, here, :] = fi
            rounded_ref[0, here, :] = fr.astype(bf16)
            rounded_ref[1, here, :] = fi.astype(bf16)

    @pl.when(pl.program_id(0) > 0)
    def _():
        @pl.loop(0, feeds // ROWS)
        def _(block):
            here = pl.ds(pl.multiple_of(block * ROWS, ROWS), ROWS)
            hr, hi = times(high_ref[0, here, :], high_ref[1, here, :], stride_ref[0, here, :], stride_ref[1, here, :])
            high_ref[0, here, :] = hr
            high_ref[1, here, :] = hi
            rounded_ref[0, here, :] = hr.astype(bf16)
            rounded_ref[1, here, :] = hi.astype(bf16)

    for j in range(width):
        total = jnp.zeros((rows, 2 * beams), jnp.float32)
        for begin in range(0, feeds, DEPTH):
            here = slice(begin, begin + DEPTH)
            wr, wi = times(rounded_ref[0, here, :], rounded_ref[1, here, :], low_ref[j, 0, here, :], low_ref[j, 1, here, :])
            weights = jnp.concatenate([wr, wi], axis=1)
            total = total + jnp.dot(v_ref[j, :, here], weights, preferred_element_type=jnp.float32)
        upper, lower = total[:half], total[half:]
        real_part = upper[:, :beams] - lower[:, beams:]
        imag_part = upper[:, beams:] + lower[:, :beams]
        out_ref[j] = (jnp.concatenate([real_part, imag_part], axis=0) * scale).astype(bf16)


def beamform(turned, first, unit):
    chan_count, rows, feeds = turned.shape
    beams = first.shape[2]
    width = math.gcd(chan_count, 16)
    table = pl.BlockSpec((2, feeds, beams), lambda i: (0, 0, 0))
    return pl.pallas_call(
        functools.partial(beam_kernel, 1.0 / math.sqrt(feeds)),
        grid=(chan_count // width,),
        out_shape=jax.ShapeDtypeStruct((chan_count, rows, beams), jnp.bfloat16),
        in_specs=[pl.BlockSpec((width, rows, feeds), lambda i: (i, 0, 0)), table, table],
        out_specs=pl.BlockSpec((width, rows, beams), lambda i: (i, 0, 0)),
        scratch_shapes=[
            pltpu.VMEM((width, 2, feeds, beams), jnp.bfloat16),
            pltpu.VMEM((2, feeds, beams), jnp.float32),
            pltpu.VMEM((2, feeds, beams), jnp.float32),
            pltpu.VMEM((2, feeds, beams), jnp.bfloat16),
        ],
        compiler_params=pltpu.CompilerParams(vmem_limit_bytes=40 * 1024 * 1024),
    )(turned, first, unit)


def make_basis(size):
    width = math.gcd(size, 32)
    columns = lax.iota(jnp.int32, size)
    low = turn(lax.iota(jnp.int32, width)[:, None] * columns[None, :], size)
    high = turn(width * lax.iota(jnp.int32, size // width)[:, None] * columns[None, :], size)
    cosine, sine = times(high[0][:, None, :], high[1][:, None, :], low[0][None], low[1][None])
    cosine = cosine.reshape(size, size).astype(jnp.bfloat16)
    sine = sine.reshape(size, size).astype(jnp.bfloat16)
    upper = jnp.concatenate([cosine, sine], axis=1)
    lower = jnp.concatenate([-sine, cosine], axis=1)
    return jnp.stack([upper, lower])


def synthesize(beamed, basis):
    size = basis.shape[1]
    frames = jnp.einsum("bstc,scn->tbn", beamed, basis, preferred_element_type=jnp.float32)
    return (frames * (1.0 / math.sqrt(size))).astype(jnp.bfloat16)


def apply_taps(extended, synthesis_taps):
    taps, size = synthesis_taps.shape
    frame_count = extended.shape[0] - (taps - 1)
    widened = extended.astype(jnp.float32)
    doubled = jnp.concatenate([synthesis_taps, synthesis_taps], axis=1)
    total = jnp.zeros((frame_count,) + extended.shape[1:], jnp.float32)
    for tap_index in range(taps):
        begin = taps - 1 - tap_index
        total = total + doubled[tap_index][None, None, :] * widened[begin : begin + frame_count]
    output = total.astype(jnp.bfloat16).reshape(frame_count, extended.shape[1], 2, size)
    return jnp.transpose(output, (2, 1, 0, 3))


def on_device(voltages, feed_position, beam_steering, synthesis_taps):
    devices_chan = lax.axis_size("chan")
    size = voltages.shape[3]
    frame_count = voltages.shape[1]
    taps = synthesis_taps.shape[0]
    chan_count = size // devices_chan
    chan_start = lax.axis_index("chan") * chan_count
    delays = compute_delays(feed_position, beam_steering)
    first = turn(chan_start * delays, PHASES)
    unit = turn(delays, PHASES)
    turned = lax.all_to_all(voltages, "chan", split_axis=3, concat_axis=2, tiled=True)
    feeds = turned.shape[2]
    turned = jnp.transpose(turned.reshape(2 * frame_count, feeds, chan_count), (2, 0, 1))
    beamed = jnp.transpose(beamform(turned, first, unit), (2, 1, 0))
    regrouped = lax.all_to_all(beamed, "chan", split_axis=0, concat_axis=2, tiled=True)
    regrouped = regrouped.reshape(regrouped.shape[0], 2, frame_count, size)
    basis = make_basis(size)
    frames = synthesize(regrouped, basis)
    carried = passed_along(frames[frame_count - (taps - 1) :], "tm", 1)
    extended = jnp.concatenate([carried, frames], axis=0)
    return apply_taps(extended, synthesis_taps)


def solution(mesh):
    return jax.shard_map(
        on_device,
        mesh=mesh,
        in_specs=(P(None, ("group", "tm"), "chan", None), P(), P("group", None), P()),
        out_specs=P(None, "chan", ("group", "tm"), None),
        check_vma=False,
    )
```

time: 708 us -> 155 us (0.22)
  other arithmetic: 591 us -> 17 us
  matrix products: 54.3 us -> 4.29 us
  Pallas kernels: 0 us -> 39.7 us
  waiting for transfers between devices: 25.6 us -> 47.7 us
  local copies, waits for them, and re-layouts: 20.9 us -> 32.7 us
    another operation x35 -> x2, other arithmetic: 579 us -> 6.86 us  [the longest x1 6.72 us: make_basis(): return jnp.stack([upper, lower])]
    dot_general x33 -> x1, matrix products: 54.3 us -> 4.29 us  [synthesize(): jnp.einsum('bstc,scn->tbn', beamed, basis, preferred_element_type=jnp.flo...]
    pallas_call x0 -> x1, Pallas kernels: none -> 39.7 us  [beamform(): pl.pallas_call(functools.partial(beam_kernel, 1.0 / math.sqrt(feeds)), gr...]
    all_to_all x1, waiting for transfers between devices: 15.2 us -> 37.5 us  [on_device(): lax.all_to_all(voltages, 'chan', split_axis=3, concat_axis=2, tiled=True)]
    select_n x32 -> x0, other arithmetic: 10.9 us -> none  [compute_delays(): return (first + second) % PHASES]
    reshape x2 -> x4, local copies, waits for them, and re-layouts: 1.58 us -> 9.66 us  [the longest x1 7.72 us: on_device(): turned.reshape(2 * frame_count, feeds, chan_count)]
  transfers between devices with their start and end apart: 3 -> 3, of which waited for: 3 -> 3; matrix products, arithmetic and copies ran while one was open for 6% -> 11% of each run, Pallas kernels for 0% -> 0%
where the time goes in v1:
time: 155 us; the launch traced here: 154 us
  waiting for transfers between devices  47.7 us (31%)
  Pallas kernels  39.7 us (26%)
  local copies, waits for them, and re-layouts  32.7 us (21%)
  other arithmetic  17 us (11%)
  starting transfers between devices  12.8 us (8%)
  matrix products  4.29 us (3%)
    pallas_call x1, Pallas kernels, beamform(): pl.pallas_call(functools.partial(beam_kernel, 1.0 / math.sqrt(feeds)), gr...  39.7 us
    all_to_all x1, waiting for transfers between devices, on_device(): lax.all_to_all(voltages, 'chan', split_axis=3, concat_axis=2, tiled=True)  37.5 us
    unnamed x12, local copies, waits for them, and re-layouts  11.4 us
    all_to_all x1, local copies, waits for them, and re-layouts, on_device(): lax.all_to_all(voltages, 'chan', split_axis=3, concat_axis=2, tiled=True)  9.74 us
    ppermute x1, waiting for transfers between devices, passed_along(): lax.ppermute(value, axis, [(source, source + steps) for source in range(i...  8.1 us
    reshape x1, local copies, waits for them, and re-layouts, on_device(): turned.reshape(2 * frame_count, feeds, chan_count)  7.72 us
    another operation x1, other arithmetic, make_basis(): return jnp.stack([upper, lower])  6.72 us
    all_to_all x1, starting transfers between devices, on_device(): lax.all_to_all(voltages, 'chan', split_axis=3, concat_axis=2, tiled=True)  4.99 us
  transfers between devices with their start and end apart: 3, of which 3 were waited for; matrix products, arithmetic and copies ran while one was open for 11% of the time, Pallas kernels for 0%

profile of v1, /device:TPU:0, one launch (start us, length us, event | category | flops | bytes accessed | tf_op | source)
XLA Modules:
  0.0 154.3 jit_solution(18202938997270790039)
XLA Ops:
  0.0 7.9 %copy.19 = bf16[2,4,256,1024]{2,1,0,3:T(4,128)(2,1)} copy(bf16[2,4,256,1024]{3,2,1,0:T(8,128)(2,1)} %param.4) | data formatting | bytes 8388608 | tf_op args[0]
  7.9 0.0 copy-start.2
  7.9 0.0 copy-start.4
  7.9 5.0 %all-to-all-start = ((bf16[2,4,256,1024]{2,1,0,3:T(4,128)(2,1)}), bf16[2,4,256,1024]{2,1,0,3:T(4,128)(2,1)}, u32[]{:S(2)}, u32[]{:S(2)}) async-start(bf16[2,4,256,1024]{2,1,0,3:T(4,128)(2,1)} %copy.19), calls=%async_computation | async-start | bytes 8388608 | tf_op jit(solution)/shard_map/all_to_all | solution.py:149
  12.9 0.0 copy-done.2
  12.9 0.5 fusion.44
  13.5 0.0 copy-done.4
  13.5 0.0 copy-done.3
  13.5 4.4 %fusion.29 = (f32[1,1024,128]{2,1,0:T(8,128)S(1)}, f32[1,1024,128]{2,1,0:T(8,128)S(1)}, f32[1,1024,128]{2,1,0:T(8,128)S(1)}, f32[1,1024,128]{2,1,0:T(8,128)S(1)}) fusion(s32[128]{0:T(128)S(1)} %get-tuple-element.20, s32[1024]{0:T(1024)S(1)} %bitcast.71, s32[128]{0:T(128)S(1)} %get-tuple-element.19, s32[1024]{0:T(1024)S(1)} %bitcast.70, s32[]{:T(128)S(6)} %mul.396), kind=kLoop, calls=%fused_computation.43 | loop fusion | flops 5373952 | bytes 2106372 | tf_op jit(solution)/shard_map/cos | solution.py:30
  17.9 0.1 pad_maximum_fusion
  18.0 0.6 fusion.47
  18.6 2.7 %add_convert_fusion = (bf16[32,32,1024]{2,1,0:T(8,128)(2,1)S(1)}, bf16[32,32,1024]{2,1,0:T(8,128)(2,1)}) fusion(f32[32,1024]{1,0:T(8,128)S(1)} %get-tuple-element.25, f32[32,1024]{1,0:T(8,128)S(1)} %get-tuple-element.22, f32[32,1024]{1,0:T(8,128)S(1)} %get-tuple-element.26, f32[32,1024]{1,0:T(8,128)S(1)} %get-tuple-element.21), kind=kLoop, calls=%fused_computation.8 | loop fusion | flops 8388608 | bytes 4718592 | tf_op jit(solution)/shard_map/convert_element_type | solution.py:114
  21.3 1.3 copy-done.1
  22.6 1.6 %bitcast_negate_fusion = bf16[1024,1024]{1,0:T(8,128)(2,1)} fusion(bf16[32,32,1024]{2,1,0:T(8,128)(2,1)S(1)} %get-tuple-element.7), kind=kLoop, calls=%fused_computation.74 | loop fusion | flops 1048576 | bytes 4194304 | tf_op jit(solution)/shard_map/neg | solution.py:116
  24.2 37.5 %all-to-all-done = bf16[2,4,256,1024]{2,1,0,3:T(4,128)(2,1)} async-done(((bf16[2,4,256,1024]{2,1,0,3:T(4,128)(2,1)}), bf16[2,4,256,1024]{2,1,0,3:T(4,128)(2,1)}, u32[]{:S(2)}, u32[]{:S(2)}) %all-to-all-start) | async-done | bytes 4194336 | tf_op jit(solution)/shard_map/all_to_all | solution.py:149
  61.7 9.7 %copy.28 = bf16[2,4,256,4,256]{2,3,1,0,4:T(4,128)(2,1)} copy(bf16[2,4,256,4,256]{2,1,0,4,3:T(4,128)(2,1)} %bitcast.6) | data formatting | bytes 8388608 | tf_op jit(solution)/shard_map/all_to_all | solution.py:149
  71.5 7.7 %reshape.674 = bf16[8,1024,256]{1,0,2:T(8,128)(2,1)} reshape(bf16[2,4,4,256,256]{3,2,1,0,4:T(4,128)(2,1)} %bitcast.63) | data formatting | bytes 8388608 | tf_op jit(solution)/shard_map/reshape | solution.py:151
  79.2 2.2 %copy-done = bf16[8,1024,256]{1,0,2:T(8,128)(2,1)S(1)} copy-done((bf16[8,1024,256]{1,0,2:T(8,128)(2,1)S(1)}, bf16[8,1024,256]{1,0,2:T(8,128)(2,1)}, u32[]{:S(2)}) %copy-start) | copy-done | bytes 4194328
  81.4 39.7 %shard_map.46 = bf16[256,8,128]{2,1,0:T(8,128)(2,1)S(1)} custom-call(bf16[256,8,1024]{2,1,0:T(8,128)(2,1)S(1)} %bitcast.60, f32[2,1024,128]{2,1,0:T(8,128)S(1)} %get-tuple-element.23.first_ref, f32[2,1024,128]{2,1,0:T(8,128)S(1)} %get-tuple-element.24.unit_ref), custom_call_target="tpu_custom_call" | custom-call | tf_op jit(solution)/shard_map/pallas_call | solution.py:91
  121.1 1.4 copy.21
  122.5 3.5 %all-to-all-start.1 = ((bf16[128,8,256]{2,1,0:T(8,128)(2,1)}), bf16[128,8,256]{2,1,0:T(8,128)(2,1)S(1)}, u32[]{:S(2)}, u32[]{:S(2)}) async-start(bf16[128,8,256]{2,1,0:T(8,128)(2,1)} %copy.21), calls=%async_computation.1 | async-start | bytes 1048576 | tf_op jit(solution)/shard_map/all_to_all | solution.py:153
  126.0 6.7 %maximum_bitcast_fusion = (bf16[1,1024,2048]{2,1,0:T(8,128)(2,1)}, bf16[1,1024,2048]{2,1,0:T(8,128)(2,1)}) fusion(bf16[1024,1024]{1,0:T(8,128)(2,1)} %bitcast.62, bf16[1024,1024]{1,0:T(8,128)(2,1)} %bitcast.64, bf16[1024,1024]{1,0:T(8,128)(2,1)} %bitcast_negate_fusion), kind=kLoop, calls=%fused_computation.5 | loop fusion | flops 16777216 | bytes 14680064 | tf_op jit(solution)/shard_map/stack | solution.py:117
  132.7 2.1 %all-to-all-done.1 = bf16[128,8,256]{2,1,0:T(8,128)(2,1)S(1)} async-done(((bf16[128,8,256]{2,1,0:T(8,128)(2,1)}), bf16[128,8,256]{2,1,0:T(8,128)(2,1)S(1)}, u32[]{:S(2)}, u32[]{:S(2)}) %all-to-all-start.1) | async-done | bytes 524320 | tf_op jit(solution)/shard_map/all_to_all | solution.py:153
  134.8 0.4 copy.22
  135.2 0.4 reshape.675
  135.6 4.3 %fusion.14 = bf16[4,32,2048]{2,1,0:T(8,128)(2,1)S(1)} fusion(bf16[32,2,4,1024]{3,0,2,1:T(8,128)(2,1)S(1)} %reshape.675, bf16[1,1024,2048]{2,1,0:T(8,128)(2,1)} %get-tuple-element.6, bf16[1,1024,2048]{2,1,0:T(8,128)(2,1)} %get-tuple-element.5), kind=kOutput, calls=%fused_computation.13 | convolution fusion | flops 1091043328 | bytes 9437184 | tf_op jit(solution)/shard_map/bstc,scn->tbn/dot_general | solution.py:122
  139.9 4.3 %collective-permute-start = (bf16[3,32,2048]{2,1,0:T(8,128)(2,1)S(1)}, bf16[3,32,2048]{2,1,0:T(8,128)(2,1)S(1)}, u32[]{:S(2)}, u32[]{:S(2)}) collective-permute-start(bf16[3,32,2048]{2,1,0:T(8,128)(2,1)S(1)} %slice.53), channel_id=1, source_target_pairs={{0,1},{1,2},{2,3},{4,5},{5,6},{6,7},{8,9},{9,10},{10,11},{12,13},{... | collective-permute-start | bytes 1179656 | tf_op jit(solution)/shard_map/ppermute | solution.py:19
  144.3 8.1 %collective-permute-done = bf16[3,32,2048]{2,1,0:T(8,128)(2,1)S(1)} collective-permute-done((bf16[3,32,2048]{2,1,0:T(8,128)(2,1)S(1)}, bf16[3,32,2048]{2,1,0:T(8,128)(2,1)S(1)}, u32[]{:S(2)}, u32[]{:S(2)}) %collective-permute-start) | collective-permute-done | bytes 393248 | tf_op jit(solution)/shard_map/ppermute | solution.py:19
  152.4 0.1 maximum_convert_fusion
  152.5 0.3 fusion.18
  152.8 0.4 reshape.676
  153.1 1.2 copy.29
  (10 shorter events, 0.1 us)
Async XLA Ops:
  7.9 5.0 %copy-start.2 = (f32[4,1024]{1,0:T(4,128)S(1)}, f32[4,1024]{1,0:T(4,128)}, u32[]{:S(2)}) copy-start(f32[4,1024]{1,0:T(4,128)} %param.7) | copy-start | bytes 49156
  7.9 5.6 %copy-start.4 = (s32[128,2]{0,1:T(2,128)S(1)}, s32[128,2]{0,1:T(2,128)}, u32[]{:S(2)}) copy-start(s32[128,2]{0,1:T(2,128)} %param.6) | copy-start | bytes 3076
  7.9 5.6 %copy-start.3 = (s32[1024,2]{0,1:T(2,128)S(1)}, s32[1024,2]{0,1:T(2,128)}, u32[]{:S(2)}) copy-start(s32[1024,2]{0,1:T(2,128)} %param.5) | copy-start | bytes 24580
  7.9 53.8 %all-to-all-start = ((bf16[2,4,256,1024]{2,1,0,3:T(4,128)(2,1)}), bf16[2,4,256,1024]{2,1,0,3:T(4,128)(2,1)}, u32[]{:S(2)}, u32[]{:S(2)}) async-start(bf16[2,4,256,1024]{2,1,0,3:T(4,128)(2,1)} %copy.19), calls=%async_computation | async-start | bytes 8388608 | tf_op jit(solution)/shard_map/all_to_all | solution.py:149
  21.3 1.3 copy-start.1
  79.2 2.2 %copy-start = (bf16[8,1024,256]{1,0,2:T(8,128)(2,1)S(1)}, bf16[8,1024,256]{1,0,2:T(8,128)(2,1)}, u32[]{:S(2)}) copy-start(bf16[8,1024,256]{1,0,2:T(8,128)(2,1)} %reshape.674) | copy-start | bytes 12582916
  122.5 12.3 %all-to-all-start.1 = ((bf16[128,8,256]{2,1,0:T(8,128)(2,1)}), bf16[128,8,256]{2,1,0:T(8,128)(2,1)S(1)}, u32[]{:S(2)}, u32[]{:S(2)}) async-start(bf16[128,8,256]{2,1,0:T(8,128)(2,1)} %copy.21), calls=%async_computation.1 | async-start | bytes 1048576 | tf_op jit(solution)/shard_map/all_to_all | solution.py:153
  139.9 12.5 %collective-permute-start = (bf16[3,32,2048]{2,1,0:T(8,128)(2,1)S(1)}, bf16[3,32,2048]{2,1,0:T(8,128)(2,1)S(1)}, u32[]{:S(2)}, u32[]{:S(2)}) collective-permute-start(bf16[3,32,2048]{2,1,0:T(8,128)(2,1)S(1)} %slice.53), channel_id=1, source_target_pairs={{0,1},{1,2},{2,3},{4,5},{5,6},{6,7},{8,9},{9,10},{10,11},{12,13},{... | collective-permute-start | bytes 1179656 | tf_op jit(solution)/shard_map/ppermute | solution.py:19

commit v2 on v1

--- a/solution.py
+++ b/solution.py
@@ -10,7 +10,8 @@
 
 PHASES = 4096
 ROWS = 32
-DEPTH = 256
+CHUNKS = 4
+WIDTH = 8
 
 
 def passed_along(value, axis, steps):
@@ -35,7 +36,8 @@
 
 
 def beam_kernel(scale, v_ref, first_ref, unit_ref, out_ref, low_ref, high_ref, stride_ref, rounded_ref):
-    width, rows, feeds = v_ref.shape
+    sources, width, rows, depth = v_ref.shape
+    feeds = sources * depth
     half = rows // 2
     beams = first_ref.shape[2]
     bf16 = jnp.bfloat16
@@ -72,11 +74,11 @@
 
     for j in range(width):
         total = jnp.zeros((rows, 2 * beams), jnp.float32)
-        for begin in range(0, feeds, DEPTH):
-            here = slice(begin, begin + DEPTH)
+        for source in range(sources):
+            here = slice(source * depth, (source + 1) * depth)
             wr, wi = times(rounded_ref[0, here, :], rounded_ref[1, here, :], low_ref[j, 0, here, :], low_ref[j, 1, here, :])
             weights = jnp.concatenate([wr, wi], axis=1)
-            total = total + jnp.dot(v_ref[j, :, here], weights, preferred_element_type=jnp.float32)
+            total = total + jnp.dot(v_ref[source, j], weights, preferred_element_type=jnp.float32)
         upper, lower = total[:half], total[half:]
         real_part = upper[:, :beams] - lower[:, beams:]
         imag_part = upper[:, beams:] + lower[:, :beams]
@@ -84,15 +86,16 @@
 
 
 def beamform(turned, first, unit):
-    chan_count, rows, feeds = turned.shape
+    sources, chan_count, rows, depth = turned.shape
+    feeds = sources * depth
     beams = first.shape[2]
-    width = math.gcd(chan_count, 16)
+    width = math.gcd(chan_count, WIDTH)
     table = pl.BlockSpec((2, feeds, beams), lambda i: (0, 0, 0))
     return pl.pallas_call(
         functools.partial(beam_kernel, 1.0 / math.sqrt(feeds)),
         grid=(chan_count // width,),
         out_shape=jax.ShapeDtypeStruct((chan_count, rows, beams), jnp.bfloat16),
-        in_specs=[pl.BlockSpec((width, rows, feeds), lambda i: (i, 0, 0)), table, table],
+        in_specs=[pl.BlockSpec((sources, width, rows, depth), lambda i: (0, i, 0, 0)), table, table],
         out_specs=pl.BlockSpec((width, rows, beams), lambda i: (i, 0, 0)),
         scratch_shapes=[
             pltpu.VMEM((width, 2, feeds, beams), jnp.bfloat16),
@@ -100,6 +103,11 @@
             pltpu.VMEM((2, feeds, beams), jnp.float32),
             pltpu.VMEM((2, feeds, beams), jnp.bfloat16),
         ],
+        cost_estimate=pl.CostEstimate(
+            flops=8 * chan_count * rows * feeds * beams,
+            bytes_accessed=2 * turned.size + 16 * feeds * beams,
+            transcendentals=0,
+        ),
         compiler_params=pltpu.CompilerParams(vmem_limit_bytes=40 * 1024 * 1024),
     )(turned, first, unit)
 
@@ -112,15 +120,15 @@
     cosine, sine = times(high[0][:, None, :], high[1][:, None, :], low[0][None], low[1][None])
     cosine = cosine.reshape(size, size).astype(jnp.bfloat16)
     sine = sine.reshape(size, size).astype(jnp.bfloat16)
-    upper = jnp.concatenate([cosine, sine], axis=1)
-    lower = jnp.concatenate([-sine, cosine], axis=1)
-    return jnp.stack([upper, lower])
+    return jnp.concatenate([cosine, sine], axis=1)
 
 
 def synthesize(beamed, basis):
-    size = basis.shape[1]
-    frames = jnp.einsum("bstc,scn->tbn", beamed, basis, preferred_element_type=jnp.float32)
-    return (frames * (1.0 / math.sqrt(size))).astype(jnp.bfloat16)
+    size = basis.shape[0]
+    product = jnp.einsum("bstc,cn->stbn", beamed, basis, preferred_element_type=jnp.float32)
+    real_part = product[0, ..., :size] - product[1, ..., size:]
+    imag_part = product[0, ..., size:] + product[1, ..., :size]
+    return (jnp.concatenate([real_part, imag_part], axis=-1) * (1.0 / math.sqrt(size))).astype(jnp.bfloat16)
 
 
 def apply_taps(extended, synthesis_taps):
@@ -144,12 +152,18 @@
     chan_count = size // devices_chan
     chan_start = lax.axis_index("chan") * chan_count
     delays = compute_delays(feed_position, beam_steering)
-    first = turn(chan_start * delays, PHASES)
     unit = turn(delays, PHASES)
-    turned = lax.all_to_all(voltages, "chan", split_axis=3, concat_axis=2, tiled=True)
-    feeds = turned.shape[2]
-    turned = jnp.transpose(turned.reshape(2 * frame_count, feeds, chan_count), (2, 0, 1))
-    beamed = jnp.transpose(beamform(turned, first, unit), (2, 1, 0))
+    feeds = voltages.shape[2]
+    chunks = math.gcd(chan_count, CHUNKS)
+    part = chan_count // chunks
+    turned = jnp.transpose(voltages.reshape(2 * frame_count, feeds, size), (2, 0, 1))
+    turned = lax.optimization_barrier(turned.reshape(devices_chan, chunks, part, 2 * frame_count, feeds))
+    blocks = []
+    for chunk in range(chunks):
+        received = lax.all_to_all(turned[:, chunk], "chan", split_axis=0, concat_axis=0, tiled=True)
+        first = turn((chan_start + chunk * part) * delays, PHASES)
+        blocks.append(beamform(received, first, unit))
+    beamed = jnp.transpose(jnp.concatenate(blocks, axis=0), (2, 1, 0))
     regrouped = lax.all_to_all(beamed, "chan", split_axis=0, concat_axis=2, tiled=True)
     regrouped = regrouped.reshape(regrouped.shape[0], 2, frame_count, size)
     basis = make_basis(size)

time: 155 us -> 156 us (level)
  waiting for transfers between devices: 47.7 us -> 26.3 us
  blocking collectives: 0 us -> 18.6 us
  local copies, waits for them, and re-layouts: 32.7 us -> 16 us
  Pallas kernels: 39.7 us -> 49.7 us
  other arithmetic: 17 us -> 23 us
  starting transfers between devices: 12.8 us -> 18.4 us
    all_to_all x1 -> x3, waiting for transfers between devices: 37.5 us -> 13.9 us  [on_device(): lax.all_to_all(turned[:, chunk], 'chan', split_axis=0, concat_axis=0, til...]
    all_to_all x0 -> x1, blocking collectives: none -> 18.6 us  [on_device(): lax.all_to_all(turned[:, chunk], 'chan', split_axis=0, concat_axis=0, til...]
    unnamed x12 -> x29, local copies, waits for them, and re-layouts: 11.4 us -> 1.25 us
    pallas_call x1 -> x4, Pallas kernels: 39.7 us -> 49.7 us  [beamform(): pl.pallas_call(functools.partial(beam_kernel, 1.0 / math.sqrt(feeds)), gr...]
    all_to_all x1 -> x0, local copies, waits for them, and re-layouts: 9.74 us -> none  [on_device(): lax.all_to_all(voltages, 'chan', split_axis=3, concat_axis=2, tiled=True)]
    cos x2, other arithmetic: 4.96 us -> 13.4 us  [turn(): return jnp.stack([jnp.cos(angles), jnp.sin(angles)])]
    another operation x1 -> x0, other arithmetic: 6.72 us -> none  [make_basis(): return jnp.stack([upper, lower])]
    all_to_all x1 -> x3, starting transfers between devices: 4.99 us -> 11.3 us  [on_device(): lax.all_to_all(turned[:, chunk], 'chan', split_axis=0, concat_axis=0, til...]
  transfers between devices with their start and end apart: 3 -> 5, of which waited for: 3 -> 4; matrix products, arithmetic and copies ran while one was open for 11% -> 15% of each run, Pallas kernels for 0% -> 24%
where the time goes in v2:
time: 156 us; the launch traced here: 155 us
  Pallas kernels  49.7 us (32%)
  waiting for transfers between devices  26.3 us (17%)
  other arithmetic  23 us (15%)
  blocking collectives  18.6 us (12%)
  starting transfers between devices  18.4 us (12%)
  local copies, waits for them, and re-layouts  16 us (10%)
  matrix products  2.84 us (2%)
    pallas_call x4, Pallas kernels, beamform(): pl.pallas_call(functools.partial(beam_kernel, 1.0 / math.sqrt(feeds)), gr...  49.7 us
    all_to_all x1, blocking collectives, on_device(): lax.all_to_all(turned[:, chunk], 'chan', split_axis=0, concat_axis=0, til...  18.6 us
    all_to_all x3, waiting for transfers between devices, on_device(): lax.all_to_all(turned[:, chunk], 'chan', split_axis=0, concat_axis=0, til...  13.9 us
    cos x2, other arithmetic, turn(): return jnp.stack([jnp.cos(angles), jnp.sin(angles)])  13.4 us
    all_to_all x3, starting transfers between devices, on_device(): lax.all_to_all(turned[:, chunk], 'chan', split_axis=0, concat_axis=0, til...  11.3 us
    ppermute x1, waiting for transfers between devices, passed_along(): lax.ppermute(value, axis, [(source, source + steps) for source in range(i...  8.08 us
    reshape x1, local copies, waits for them, and re-layouts, on_device(): voltages.reshape(2 * frame_count, feeds, size)  7 us
    all_to_all x1, waiting for transfers between devices, on_device(): lax.all_to_all(beamed, 'chan', split_axis=0, concat_axis=2, tiled=True)  4.32 us
  transfers between devices with their start and end apart: 5, of which 4 were waited for; matrix products, arithmetic and copies ran while one was open for 15% of the time, Pallas kernels for 24%

profile of v2, /device:TPU:0, one launch (start us, length us, event | category | flops | bytes accessed | tf_op | source)
XLA Modules:
  0.0 155.1 jit_solution(8042777435736466179)
XLA Ops:
  0.0 7.0 %copy.33 = bf16[8,256,1024]{1,0,2:T(8,128)(2,1)} copy(bf16[8,256,1024]{2,1,0:T(8,128)(2,1)} %bitcast.57) | data formatting | bytes 8388608 | tf_op jit(solution)/shard_map/reshape | solution.py:159
  7.0 3.9 %slice_bitcast_fusion.3 = (bf16[4,64,8,256]{3,2,1,0:T(8,128)(2,1)}, bf16[4,64,8,256]{3,2,1,0:T(8,128)(2,1)}, bf16[4,64,8,256]{3,2,1,0:T(8,128)(2,1)}, bf16[4,64,8,256]{3,2,1,0:T(8,128)(2,1)S(1)}) fusion(bf16[4,4,64,8,256]{4,3,2,1,0:T(8,128)(2,1)} %bitcast.56), kind=kLoop, calls=%fused_computation.18 | loop fusion | bytes 8388608 | tf_op jit(solution)/shard_map/squeeze | solution.py:163
  10.9 18.6 %all_to_all.35.v_ref = bf16[4,64,8,256]{3,2,1,0:T(8,128)(2,1)S(1)} all-to-all(bf16[4,64,8,256]{3,2,1,0:T(8,128)(2,1)S(1)} %get-tuple-element.8), channel_id=1, replica_groups=mesh['group'=2,'chan'=4,'tm'=4] {'chan'}, dimensions={0} | all-to-all | bytes 2097152 | tf_op jit(solution)/shard_map/all_to_all | solution.py:163
  29.5 3.5 %all-to-all-start.2 = ((bf16[4,64,8,256]{3,2,1,0:T(8,128)(2,1)}), bf16[4,64,8,256]{3,2,1,0:T(8,128)(2,1)S(1)}, u32[]{:S(2)}, u32[]{:S(2)}) async-start(bf16[4,64,8,256]{3,2,1,0:T(8,128)(2,1)} %get-tuple-element.6), calls=%async_computation.2 | async-start | bytes 2097152 | tf_op jit(solution)/shard_map/all_to_all | solution.py:163
  33.1 0.6 constant_dynamic-update-slice_fusion.1
  33.7 1.2 fusion.49
  34.9 12.6 %all-to-all-done.2.v_ref = bf16[4,64,8,256]{3,2,1,0:T(8,128)(2,1)S(1)} async-done(((bf16[4,64,8,256]{3,2,1,0:T(8,128)(2,1)}), bf16[4,64,8,256]{3,2,1,0:T(8,128)(2,1)S(1)}, u32[]{:S(2)}, u32[]{:S(2)}) %all-to-all-start.2) | async-done | bytes 1048608 | tf_op jit(solution)/shard_map/all_to_all | solution.py:163
  47.5 3.5 %all-to-all-start.1 = ((bf16[4,64,8,256]{3,2,1,0:T(8,128)(2,1)}), bf16[4,64,8,256]{3,2,1,0:T(8,128)(2,1)S(1)}, u32[]{:S(2)}, u32[]{:S(2)}) async-start(bf16[4,64,8,256]{3,2,1,0:T(8,128)(2,1)} %get-tuple-element.7), calls=%async_computation.1 | async-start | bytes 2097152 | tf_op jit(solution)/shard_map/all_to_all | solution.py:163
  51.0 12.1 %fusion.36 = (f32[1,1024,128]{2,1,0:T(8,128)}, f32[1,1024,128]{2,1,0:T(8,128)}, f32[1,1024,128]{2,1,0:T(8,128)}, f32[1,1024,128]{2,1,0:T(8,128)}, f32[1,1024,128...) fusion(s32[128]{0:T(128)S(1)} %get-tuple-element.30, ...), kind=kLoop, calls=%fused_computation.76 | loop fusion | flops 10878976 | bytes 5252112 | tf_op jit(solution)/shard_map/cos | solution.py:31
  63.1 1.1 pad_maximum_fusion.4.first_ref
  64.2 1.3 all-to-all-done.1.v_ref
  65.4 4.2 %all-to-all-start = ((bf16[4,64,8,256]{3,2,1,0:T(8,128)(2,1)}), bf16[4,64,8,256]{3,2,1,0:T(8,128)(2,1)}, u32[]{:S(2)}, u32[]{:S(2)}) async-start(bf16[4,64,8,256]{3,2,1,0:T(8,128)(2,1)} %get-tuple-element.5), calls=%async_computation | async-start | bytes 2097152 | tf_op jit(solution)/shard_map/all_to_all | solution.py:163
  69.8 2.8 %pad_maximum_fusion = (f32[2,1024,128]{2,1,0:T(8,128)}, f32[2,1024,128]{2,1,0:T(8,128)S(1)}) fusion(f32[1,1024,128]{2,1,0:T(8,128)} %get-tuple-element.18, f32[1,1024,128]{2,1,0:T(8,128)} %get-tuple-element.17, f32[1,1024,128]{2,1,0:T(8,128)} %get-tuple-element.22, f32[1,1024,128]{2,1,0:T(8,128)} %get-tuple-element.23), kind=kLoop, calls=%fused_computation.19 | loop fusion | flops 524288 | bytes 4194304 | tf_op jit(solution)/shard_map/stack | solution.py:31
  72.7 1.3 fusion.52
  74.0 12.2 %shard_map.49 = bf16[64,8,128]{2,1,0:T(8,128)(2,1)S(1)} custom-call(bf16[4,64,8,256]{3,2,1,0:T(8,128)(2,1)S(1)} %all_to_all.35.v_ref, f32[2,1024,128]{2,1,0:T(8,128)S(1)} %copy-done.2, f32[2,1024,128]{2,1,0:T(8,128)S(1)} %get-tuple-element.34.unit_ref), custom_call_target="tpu_custom_call" | custom-call | flops 536870912 | bytes 3145728 | tf_op jit(solution)/shard_map/pallas_call | solution.py:94
  86.3 12.2 %shard_map.48 = bf16[64,8,128]{2,1,0:T(8,128)(2,1)S(1)} custom-call(bf16[4,64,8,256]{3,2,1,0:T(8,128)(2,1)S(1)} %all-to-all-done.2.v_ref, f32[2,1024,128]{2,1,0:T(8,128)S(1)} %get-tuple-element.36.first_ref, f32[2,1024,128]{2,1,0:T(8,128)S(1)} %get-tuple-element.34.unit_ref), custom_call_target="tpu_custom_call" | custom-call | flops 536870912 | bytes 3145728 | tf_op jit(solution)/shard_map/pallas_call | solution.py:94
  98.5 12.2 %shard_map.47 = bf16[64,8,128]{2,1,0:T(8,128)(2,1)S(1)} custom-call(bf16[4,64,8,256]{3,2,1,0:T(8,128)(2,1)S(1)} %copy-done.1, f32[2,1024,128]{2,1,0:T(8,128)S(1)} %get-tuple-element.35.first_ref, f32[2,1024,128]{2,1,0:T(8,128)S(1)} %get-tuple-element.34.unit_ref), custom_call_target="tpu_custom_call" | custom-call | flops 536870912 | bytes 3145728 | tf_op jit(solution)/shard_map/pallas_call | solution.py:94
  110.8 13.0 %shard_map.46 = bf16[64,8,128]{2,1,0:T(8,128)(2,1)S(1)} custom-call(bf16[4,64,8,256]{3,2,1,0:T(8,128)(2,1)} %all-to-all-done.v_ref, f32[2,1024,128]{2,1,0:T(8,128)S(1)} %copy-done.3, f32[2,1024,128]{2,1,0:T(8,128)S(1)} %get-tuple-element.34.unit_ref), custom_call_target="tpu_custom_call" | custom-call | flops 536870912 | bytes 3145728 | tf_op jit(solution)/shard_map/pallas_call | solution.py:94
  123.9 1.4 copy.29
  125.2 3.7 %all-to-all-start.4 = ((bf16[128,8,256]{2,1,0:T(8,128)(2,1)}), bf16[128,8,256]{2,1,0:T(8,128)(2,1)S(1)}, u32[]{:S(2)}, u32[]{:S(2)}) async-start(bf16[128,8,256]{2,1,0:T(8,128)(2,1)} %copy.29), calls=%async_computation.4 | async-start | bytes 1048576 | tf_op jit(solution)/shard_map/all_to_all | solution.py:167
  128.9 0.6 copy-done.9
  129.5 3.8 %subtract_convert_fusion = (bf16[32,32,1024]{2,1,0:T(8,128)(2,1)S(1)}, bf16[32,32,1024]{2,1,0:T(8,128)(2,1)}) fusion(f32[32,1024]{1,0:T(8,128)S(1)} %get-tuple-element.37, f32[32,1024]{1,0:T(8,128)} %get-tuple-element.32, f32[32,1024]{1,0:T(8,128)} %get-tuple-element.38, f32[32,1024]{1,0:T(8,128)} %get-tuple-element.31), kind=kLoop, calls=%fused_computation.5 | loop fusion | flops 8388608 | bytes 4718592 | tf_op jit(solution)/shard_map/convert_element_type | solution.py:121
  133.3 4.3 %all-to-all-done.4 = bf16[128,8,256]{2,1,0:T(8,128)(2,1)S(1)} async-done(((bf16[128,8,256]{2,1,0:T(8,128)(2,1)}), bf16[128,8,256]{2,1,0:T(8,128)(2,1)S(1)}, u32[]{:S(2)}, u32[]{:S(2)}) %all-to-all-start.4) | async-done | bytes 524320 | tf_op jit(solution)/shard_map/all_to_all | solution.py:167
  137.6 0.4 copy.30
  138.0 0.4 reshape.1448
  138.4 2.8 %fusion.3 = f32[2,4,32,2048]{3,2,1,0:T(8,128)S(1)} fusion(bf16[32,2,4,1024]{3,0,2,1:T(8,128)(2,1)S(1)} %reshape.1448, bf16[1024,1024]{1,0:T(8,128)(2,1)} %bitcast.59, bf16[1024,1024]{1,0:T(8,128)(2,1)S(1)} %bitcast.58), kind=kOutput, calls=%fused_computation.6 | convolution fusion | flops 1082130432 | bytes 6815744 | tf_op jit(solution)/shard_map/bstc,cn->stbn/dot_general | solution.py:128
  141.3 0.2 fusion.26
  141.5 3.5 %collective-permute-start = (bf16[3,32,2048]{2,1,0:T(8,128)(2,1)S(1)}, bf16[3,32,2048]{2,1,0:T(8,128)(2,1)S(1)}, u32[]{:S(2)}, u32[]{:S(2)}) collective-permute-start(bf16[3,32,2048]{2,1,0:T(8,128)(2,1)S(1)} %slice.93), channel_id=1, source_target_pairs={{0,1},{1,2},{2,3},{4,5},{5,6},{6,7},{8,9},{9,10},{10,11},{12,13},{... | collective-permute-start | bytes 1179656 | tf_op jit(solution)/shard_map/ppermute | solution.py:20
  145.1 8.1 %collective-permute-done = bf16[3,32,2048]{2,1,0:T(8,128)(2,1)S(1)} collective-permute-done((bf16[3,32,2048]{2,1,0:T(8,128)(2,1)S(1)}, bf16[3,32,2048]{2,1,0:T(8,128)(2,1)S(1)}, u32[]{:S(2)}, u32[]{:S(2)}) %collective-permute-start) | collective-permute-done | bytes 393248 | tf_op jit(solution)/shard_map/ppermute | solution.py:20
  153.3 0.3 fusion.5
  153.6 0.4 reshape.1449
  153.9 1.2 copy.39
  (38 shorter events, 0.5 us)
Async XLA Ops:
  10.9 22.1 %copy-start.11 = (f32[4,1024]{1,0:T(4,128)S(1)}, f32[4,1024]{1,0:T(4,128)}, u32[]{:S(2)}) copy-start(f32[4,1024]{1,0:T(4,128)} %param.7) | copy-start | bytes 49156
  10.9 23.9 %copy-start.12 = (s32[1024,2]{0,1:T(2,128)S(1)}, s32[1024,2]{0,1:T(2,128)}, u32[]{:S(2)}) copy-start(s32[1024,2]{0,1:T(2,128)} %param.5) | copy-start | bytes 24580
  10.9 40.1 %copy-start.13 = (s32[128,2]{0,1:T(2,128)S(1)}, s32[128,2]{0,1:T(2,128)}, u32[]{:S(2)}) copy-start(s32[128,2]{0,1:T(2,128)} %param.6) | copy-start | bytes 3076
  29.5 18.0 %all-to-all-start.2 = ((bf16[4,64,8,256]{3,2,1,0:T(8,128)(2,1)}), bf16[4,64,8,256]{3,2,1,0:T(8,128)(2,1)S(1)}, u32[]{:S(2)}, u32[]{:S(2)}) async-start(bf16[4,64,8,256]{3,2,1,0:T(8,128)(2,1)} %get-tuple-element.6), calls=%async_computation.2 | async-start | bytes 2097152 | tf_op jit(solution)/shard_map/all_to_all | solution.py:163
  47.5 18.0 %all-to-all-start.1 = ((bf16[4,64,8,256]{3,2,1,0:T(8,128)(2,1)}), bf16[4,64,8,256]{3,2,1,0:T(8,128)(2,1)S(1)}, u32[]{:S(2)}, u32[]{:S(2)}) async-start(bf16[4,64,8,256]{3,2,1,0:T(8,128)(2,1)} %get-tuple-element.7), calls=%async_computation.1 | async-start | bytes 2097152 | tf_op jit(solution)/shard_map/all_to_all | solution.py:163
  65.4 4.3 %copy-start = (bf16[4,64,8,256]{3,2,1,0:T(8,128)(2,1)}, bf16[4,64,8,256]{3,2,1,0:T(8,128)(2,1)S(1)}, u32[]{:S(2)}) copy-start(bf16[4,64,8,256]{3,2,1,0:T(8,128)(2,1)S(1)} %all-to-all-done.1.v_ref) | copy-start | bytes 3145732
  65.4 45.3 %all-to-all-start = ((bf16[4,64,8,256]{3,2,1,0:T(8,128)(2,1)}), bf16[4,64,8,256]{3,2,1,0:T(8,128)(2,1)}, u32[]{:S(2)}, u32[]{:S(2)}) async-start(bf16[4,64,8,256]{3,2,1,0:T(8,128)(2,1)} %get-tuple-element.5), calls=%async_computation | async-start | bytes 2097152 | tf_op jit(solution)/shard_map/all_to_all | solution.py:163
  69.7 2.9 %copy-start.4 = (f32[1,1024,128]{2,1,0:T(8,128)S(1)}, f32[1,1024,128]{2,1,0:T(8,128)}, u32[]{:S(2)}) copy-start(f32[1,1024,128]{2,1,0:T(8,128)} %get-tuple-element.19) | copy-start | bytes 1572868
  69.7 2.9 %copy-start.5 = (f32[1,1024,128]{2,1,0:T(8,128)S(1)}, f32[1,1024,128]{2,1,0:T(8,128)}, u32[]{:S(2)}) copy-start(f32[1,1024,128]{2,1,0:T(8,128)} %get-tuple-element.20) | copy-start | bytes 1572868
  69.7 2.9 %copy-start.6 = (f32[1,1024,128]{2,1,0:T(8,128)S(1)}, f32[1,1024,128]{2,1,0:T(8,128)}, u32[]{:S(2)}) copy-start(f32[1,1024,128]{2,1,0:T(8,128)} %get-tuple-element.25) | copy-start | bytes 1572868
  69.7 2.8 %copy-start.7 = (f32[1,1024,128]{2,1,0:T(8,128)S(1)}, f32[1,1024,128]{2,1,0:T(8,128)}, u32[]{:S(2)}) copy-start(f32[1,1024,128]{2,1,0:T(8,128)} %get-tuple-element.26) | copy-start | bytes 1572868
  69.8 4.3 %copy-start.2 = (f32[2,1024,128]{2,1,0:T(8,128)S(1)}, f32[2,1024,128]{2,1,0:T(8,128)}, u32[]{:S(2)}) copy-start(f32[2,1024,128]{2,1,0:T(8,128)} %pad_maximum_fusion.4.first_ref) | copy-start | bytes 3145732
  72.7 25.8 %copy-start.1 = (bf16[4,64,8,256]{3,2,1,0:T(8,128)(2,1)S(1)}, bf16[4,64,8,256]{3,2,1,0:T(8,128)(2,1)}, u32[]{:S(2)}) copy-start(bf16[4,64,8,256]{3,2,1,0:T(8,128)(2,1)} %copy-done) | copy-start | bytes 3145732
  86.3 24.5 %copy-start.3 = (f32[2,1024,128]{2,1,0:T(8,128)S(1)}, f32[2,1024,128]{2,1,0:T(8,128)}, u32[]{:S(2)}) copy-start(f32[2,1024,128]{2,1,0:T(8,128)} %get-tuple-element.33.first_ref) | copy-start | bytes 3145732
  98.5 30.4 %copy-start.8 = (f32[4,2048]{1,0:T(4,128)S(1)}, f32[4,2048]{1,0:T(4,128)}, u32[]{:S(2)}) copy-start(f32[4,2048]{1,0:T(4,128)} %constant_dynamic-update-slice_fusion.1) | copy-start | bytes 98308
  125.2 12.4 %all-to-all-start.4 = ((bf16[128,8,256]{2,1,0:T(8,128)(2,1)}), bf16[128,8,256]{2,1,0:T(8,128)(2,1)S(1)}, u32[]{:S(2)}, u32[]{:S(2)}) async-start(bf16[128,8,256]{2,1,0:T(8,128)(2,1)} %copy.29), calls=%async_computation.4 | async-start | bytes 1048576 | tf_op jit(solution)/shard_map/all_to_all | solution.py:167
  128.9 0.6 copy-start.9
  141.2 3.8 %copy-start.10 = (f32[4,2048]{1,0:T(4,128)S(1)}, f32[4,2048]{1,0:T(4,128)}, u32[]{:S(2)}) copy-start(f32[4,2048]{1,0:T(4,128)} %copy-done.9) | copy-start | bytes 98308
  141.5 11.6 %collective-permute-start = (bf16[3,32,2048]{2,1,0:T(8,128)(2,1)S(1)}, bf16[3,32,2048]{2,1,0:T(8,128)(2,1)S(1)}, u32[]{:S(2)}, u32[]{:S(2)}) collective-permute-start(bf16[3,32,2048]{2,1,0:T(8,128)(2,1)S(1)} %slice.93), channel_id=1, source_target_pairs={{0,1},{1,2},{2,3},{4,5},{5,6},{6,7},{8,9},{9,10},{10,11},{12,13},{... | collective-permute-start | bytes 1179656 | tf_op jit(solution)/shard_map/ppermute | solution.py:20

commit v3 on v2

--- a/solution.py
+++ b/solution.py
@@ -158,15 +158,38 @@
     part = chan_count // chunks
     turned = jnp.transpose(voltages.reshape(2 * frame_count, feeds, size), (2, 0, 1))
     turned = lax.optimization_barrier(turned.reshape(devices_chan, chunks, part, 2 * frame_count, feeds))
+    first = turn(chan_start * delays, PHASES)
+    stride, left = unit, part
+    total = None
+    while left:
+        if left % 2:
+            total = stride if total is None else jnp.stack(times(*total, *stride))
+        left //= 2
+        stride = jnp.stack(times(*stride, *stride))
+    firsts = [first]
+    for _ in range(1, chunks):
+        firsts.append(jnp.stack(times(*firsts[-1], *total)))
+    basis = make_basis(size)
     blocks = []
     for chunk in range(chunks):
+        if chunk == 1:
+            turned, unit, firsts = lax.optimization_barrier((turned, unit, firsts))
+        if chunk == 2:
+            turned, basis = lax.optimization_barrier((turned, basis))
+        if chunk > 1:
+            turned, blocks[chunk - 2] = lax.optimization_barrier((turned, blocks[chunk - 2]))
+        if chunk > 0:
+            received, start = blocks[chunk - 1]
+            turned, received = lax.optimization_barrier((turned, received))
+            blocks[chunk - 1] = (received, start)
         received = lax.all_to_all(turned[:, chunk], "chan", split_axis=0, concat_axis=0, tiled=True)
-        first = turn((chan_start + chunk * part) * delays, PHASES)
-        blocks.append(beamform(received, first, unit))
+        blocks.append((received, firsts[chunk]))
+        if chunk > 0:
+            blocks[chunk - 1] = beamform(*blocks[chunk - 1], unit)
+    blocks[-1] = beamform(*blocks[-1], unit)
     beamed = jnp.transpose(jnp.concatenate(blocks, axis=0), (2, 1, 0))
     regrouped = lax.all_to_all(beamed, "chan", split_axis=0, concat_axis=2, tiled=True)
     regrouped = regrouped.reshape(regrouped.shape[0], 2, frame_count, size)
-    basis = make_basis(size)
     frames = synthesize(regrouped, basis)
     carried = passed_along(frames[frame_count - (taps - 1) :], "tm", 1)
     extended = jnp.concatenate([carried, frames], axis=0)

time: 156 us -> 139 us (0.89)
  blocking collectives: 18.6 us -> 0 us
  other arithmetic: 23 us -> 13.9 us
  local copies, waits for them, and re-layouts: 16 us -> 22.4 us
  starting transfers between devices: 18.4 us -> 24.1 us
  waiting for transfers between devices: 26.3 us -> 23.6 us
    all_to_all x1 -> x0, blocking collectives: 18.6 us -> none  [on_device(): lax.all_to_all(turned[:, chunk], 'chan', split_axis=0, concat_axis=0, til...]
    cos x2 -> x1, other arithmetic: 13.4 us -> 0.6 us  [turn(): return jnp.stack([jnp.cos(angles), jnp.sin(angles)])]
    all_to_all x3 -> x4, waiting for transfers between devices: 13.9 us -> 6.69 us  [on_device(): lax.all_to_all(turned[:, chunk], 'chan', split_axis=0, concat_axis=0, til...]
    sub x0 -> x1, other arithmetic: none -> 5.44 us  [times(): return (ar * br - ai * bi, ar * bi + ai * br)]
    squeeze x1 -> x4, local copies, waits for them, and re-layouts: 3.92 us -> 9.21 us  [on_device(): turned[:, chunk]]
    all_to_all x3 -> x4, starting transfers between devices: 11.3 us -> 16.4 us  [on_device(): lax.all_to_all(turned[:, chunk], 'chan', split_axis=0, concat_axis=0, til...]
    all_to_all x1, waiting for transfers between devices: 4.32 us -> 8.78 us  [on_device(): lax.all_to_all(beamed, 'chan', split_axis=0, concat_axis=2, tiled=True)]
    another operation x3 -> x1, other arithmetic: 4 us -> 1.13 us  [turn(): return jnp.stack([jnp.cos(angles), jnp.sin(angles)])]
  transfers between devices with their start and end apart: 5 -> 6, of which waited for: 4 -> 5; matrix products, arithmetic and copies ran while one was open for 15% -> 10% of each run, Pallas kernels for 24% -> 27%
where the time goes in v3:
time: 139 us; the launch traced here: 138 us
  Pallas kernels  50.4 us (36%)
  starting transfers between devices  24.1 us (17%)
  waiting for transfers between devices  23.6 us (17%)
  local copies, waits for them, and re-layouts  22.4 us (16%)
  other arithmetic  13.9 us (10%)
  matrix products  3.44 us (2%)
    pallas_call x4, Pallas kernels, beamform(): pl.pallas_call(functools.partial(beam_kernel, 1.0 / math.sqrt(feeds)), gr...  50.4 us
    all_to_all x4, starting transfers between devices, on_device(): lax.all_to_all(turned[:, chunk], 'chan', split_axis=0, concat_axis=0, til...  16.4 us
    squeeze x4, local copies, waits for them, and re-layouts, on_device(): turned[:, chunk]  9.21 us
    all_to_all x1, waiting for transfers between devices, on_device(): lax.all_to_all(beamed, 'chan', split_axis=0, concat_axis=2, tiled=True)  8.78 us
    ppermute x1, waiting for transfers between devices, passed_along(): lax.ppermute(value, axis, [(source, source + steps) for source in range(i...  8.1 us
    reshape x1, local copies, waits for them, and re-layouts, on_device(): voltages.reshape(2 * frame_count, feeds, size)  6.95 us
    all_to_all x4, waiting for transfers between devices, on_device(): lax.all_to_all(turned[:, chunk], 'chan', split_axis=0, concat_axis=0, til...  6.69 us
    sub x1, other arithmetic, times(): return (ar * br - ai * bi, ar * bi + ai * br)  5.44 us
  transfers between devices with their start and end apart: 6, of which 5 were waited for; matrix products, arithmetic and copies ran while one was open for 10% of the time, Pallas kernels for 27%

profile of v3, /device:TPU:0, one launch (start us, length us, event | category | flops | bytes accessed | tf_op | source)
XLA Modules:
  0.0 138.0 jit_solution(5644376904414393843)
XLA Ops:
  0.0 6.9 %copy.33 = bf16[8,256,1024]{1,0,2:T(8,128)(2,1)} copy(bf16[8,256,1024]{2,1,0:T(8,128)(2,1)} %bitcast.56) | data formatting | bytes 8388608 | tf_op jit(solution)/shard_map/reshape | solution.py:159
  7.0 2.3 %slice_bitcast_fusion.3 = bf16[4,64,8,256]{3,2,1,0:T(8,128)(2,1)} fusion(bf16[4,4,64,8,256]{4,3,2,1,0:T(8,128)(2,1)} %bitcast.50), kind=kLoop, calls=%fused_computation.17 | loop fusion | bytes 2097152 | tf_op jit(solution)/shard_map/squeeze | solution.py:185
  9.3 4.2 %all-to-all-start = ((bf16[4,64,8,256]{3,2,1,0:T(8,128)(2,1)}), bf16[4,64,8,256]{3,2,1,0:T(8,128)(2,1)S(1)}, u32[]{:S(2)}, u32[]{:S(2)}) async-start(bf16[4,64,8,256]{3,2,1,0:T(8,128)(2,1)} %slice_bitcast_fusion.3), calls=%async_computation | async-start | bytes 2097152 | tf_op jit(solution)/shard_map/all_to_all | solution.py:185
  13.5 5.4 %multiply_subtract_fusion = (f32[1,1024,128]{2,1,0:T(8,128)S(1)}, f32[1,1024,128]{2,1,0:T(8,128)S(1)}, f32[1,1024,128]{2,1,0:T(8,128)S(1)}, f32[1,1024,128]{2,1,...) fusion(s32[128]{0:T(128)S(1)} %get-tuple-element.60, ...), kind=kLoop, calls=%fused_computation.55 | loop fusion | flops 11665408 | bytes 5252100 | tf_op jit(solution)/shard_map/sub | solution.py:35
  19.0 1.6 %pad_maximum_fusion.3 = (f32[2,1024,128]{2,1,0:T(8,128)}, f32[2,1024,128]{2,1,0:T(8,128)}) fusion(f32[1,1024,128]{2,1,0:T(8,128)S(1)} %get-tuple-element.51, f32[1,1024,128]{2,1,0:T(8,128)S(1)} %get-tuple-element.52, f32[1,1024,128]{2,1,0:T(8,128)S(1)} %get-tuple-element.49, f32[1,1024,128]{2,1,0:T(8,128)S(1)} %get-tuple-element.48), kind=kLoop, calls=%fused_computation.20 | loop fusion | flops 524288 | bytes 4194304 | tf_op jit(solution)/shard_map/stack | solution.py:171
  20.6 1.1 pad_maximum_fusion.1
  21.7 0.6 fusion.38
  22.3 5.6 %all-to-all-done.v_ref = bf16[4,64,8,256]{3,2,1,0:T(8,128)(2,1)S(1)} async-done(((bf16[4,64,8,256]{3,2,1,0:T(8,128)(2,1)}), bf16[4,64,8,256]{3,2,1,0:T(8,128)(2,1)S(1)}, u32[]{:S(2)}, u32[]{:S(2)}) %all-to-all-start) | async-done | bytes 1048608 | tf_op jit(solution)/shard_map/all_to_all | solution.py:185
  27.9 2.3 %slice_bitcast_fusion.2 = bf16[4,64,8,256]{3,2,1,0:T(8,128)(2,1)} fusion(bf16[4,4,64,8,256]{4,3,2,1,0:T(8,128)(2,1)} %bitcast.51), kind=kLoop, calls=%fused_computation.16 | loop fusion | bytes 2097152 | tf_op jit(solution)/shard_map/squeeze | solution.py:185
  30.3 4.2 %all-to-all-start.1 = ((bf16[4,64,8,256]{3,2,1,0:T(8,128)(2,1)}), bf16[4,64,8,256]{3,2,1,0:T(8,128)(2,1)}, u32[]{:S(2)}, u32[]{:S(2)}) async-start(bf16[4,64,8,256]{3,2,1,0:T(8,128)(2,1)} %slice_bitcast_fusion.2), calls=%async_computation.1 | async-start | bytes 2097152 | tf_op jit(solution)/shard_map/all_to_all | solution.py:185
  34.5 0.5 fusion.35
  35.0 1.4 %subtract_convert_fusion = (bf16[32,32,1024]{2,1,0:T(8,128)(2,1)S(1)}, bf16[32,32,1024]{2,1,0:T(8,128)(2,1)S(1)}) fusion(f32[32,1024]{1,0:T(8,128)S(1)} %get-tuple-element.67, f32[32,1024]{1,0:T(8,128)S(1)} %get-tuple-element.62, f32[32,1024]{1,0:T(8,128)S(1)} %get-tuple-element.68, f32[32,1024]{1,0:T(8,128)S(1)} %get-tuple-element.61), kind=kLoop, calls=%fused_computation.4 | loop fusion | flops 8388608 | bytes 4718592 | tf_op jit(solution)/shard_map/convert_element_type | solution.py:121
  36.4 2.5 %pad_maximum_fusion = bf16[1024,2048]{1,0:T(8,128)(2,1)} fusion(bf16[1024,1024]{1,0:T(8,128)(2,1)S(1)} %bitcast.55, bf16[1024,1024]{1,0:T(8,128)(2,1)S(1)} %bitcast.54), kind=kLoop, calls=%fused_computation | loop fusion | flops 8388608 | bytes 8388608 | tf_op jit(solution)/shard_map/concatenate | solution.py:123
  38.9 12.2 %shard_map.46 = bf16[64,8,128]{2,1,0:T(8,128)(2,1)S(1)} custom-call(bf16[4,64,8,256]{3,2,1,0:T(8,128)(2,1)S(1)} %all-to-all-done.v_ref, f32[2,1024,128]{2,1,0:T(8,128)S(1)} %copy-done.2, f32[2,1024,128]{2,1,0:T(8,128)S(1)} %get-tuple-element.27.unit_ref), custom_call_target="tpu_custom_call" | custom-call | flops 536870912 | bytes 3145728 | tf_op jit(solution)/shard_map/pallas_call | solution.py:94
  51.1 2.3 %slice_bitcast_fusion.1 = bf16[4,64,8,256]{3,2,1,0:T(8,128)(2,1)} fusion(bf16[4,4,64,8,256]{4,3,2,1,0:T(8,128)(2,1)} %bitcast.52), kind=kLoop, calls=%fused_computation.15 | loop fusion | bytes 2097152 | tf_op jit(solution)/shard_map/squeeze | solution.py:185
  53.4 3.5 %all-to-all-start.2 = ((bf16[4,64,8,256]{3,2,1,0:T(8,128)(2,1)}), bf16[4,64,8,256]{3,2,1,0:T(8,128)(2,1)S(1)}, u32[]{:S(2)}, u32[]{:S(2)}) async-start(bf16[4,64,8,256]{3,2,1,0:T(8,128)(2,1)} %slice_bitcast_fusion.1), calls=%async_computation.2 | async-start | bytes 2097152 | tf_op jit(solution)/shard_map/all_to_all | solution.py:185
  57.0 1.2 copy-done.1
  58.2 13.0 %shard_map.47 = bf16[64,8,128]{2,1,0:T(8,128)(2,1)S(1)} custom-call(bf16[4,64,8,256]{3,2,1,0:T(8,128)(2,1)} %all-to-all-done.1.v_ref, f32[2,1024,128]{2,1,0:T(8,128)S(1)} %copy-done.1, f32[2,1024,128]{2,1,0:T(8,128)S(1)} %get-tuple-element.27.unit_ref), custom_call_target="tpu_custom_call" | custom-call | flops 536870912 | bytes 3145728 | tf_op jit(solution)/shard_map/pallas_call | solution.py:94
  71.4 2.3 %slice_bitcast_fusion = bf16[4,64,8,256]{3,2,1,0:T(8,128)(2,1)} fusion(bf16[4,4,64,8,256]{4,3,2,1,0:T(8,128)(2,1)} %bitcast.53), kind=kLoop, calls=%fused_computation.14 | loop fusion | bytes 2097152 | tf_op jit(solution)/shard_map/squeeze | solution.py:185
  73.7 4.4 %all-to-all-start.3 = ((bf16[4,64,8,256]{3,2,1,0:T(8,128)(2,1)}), bf16[4,64,8,256]{3,2,1,0:T(8,128)(2,1)}, u32[]{:S(2)}, u32[]{:S(2)}) async-start(bf16[4,64,8,256]{3,2,1,0:T(8,128)(2,1)} %slice_bitcast_fusion), calls=%async_computation.3 | async-start | bytes 2097152 | tf_op jit(solution)/shard_map/all_to_all | solution.py:185
  78.1 1.2 copy-done
  79.3 12.2 %shard_map.48 = bf16[64,8,128]{2,1,0:T(8,128)(2,1)S(1)} custom-call(bf16[4,64,8,256]{3,2,1,0:T(8,128)(2,1)S(1)} %all-to-all-done.2.v_ref, f32[2,1024,128]{2,1,0:T(8,128)S(1)} %copy-done, f32[2,1024,128]{2,1,0:T(8,128)S(1)} %get-tuple-element.27.unit_ref), custom_call_target="tpu_custom_call" | custom-call | flops 536870912 | bytes 3145728 | tf_op jit(solution)/shard_map/pallas_call | solution.py:94
  91.6 0.9 all-to-all-done.3.v_ref
  92.5 13.0 %shard_map.49 = bf16[64,8,128]{2,1,0:T(8,128)(2,1)S(1)} custom-call(bf16[4,64,8,256]{3,2,1,0:T(8,128)(2,1)} %all-to-all-done.3.v_ref, f32[2,1024,128]{2,1,0:T(8,128)S(1)} %pad_maximum_fusion.5.first_ref, f32[2,1024,128]{2,1,0:T(8,128)S(1)} %get-tuple-element.27.unit_ref), custom_call_target="tpu_custom_call" | custom-call | flops 536870912 | bytes 3145728 | tf_op jit(solution)/shard_map/pallas_call | solution.py:94
  105.5 1.4 copy.29
  106.9 3.5 %all-to-all-start.4 = ((bf16[128,8,256]{2,1,0:T(8,128)(2,1)}), bf16[128,8,256]{2,1,0:T(8,128)(2,1)S(1)}, u32[]{:S(2)}, u32[]{:S(2)}) async-start(bf16[128,8,256]{2,1,0:T(8,128)(2,1)} %copy.29), calls=%async_computation.4 | async-start | bytes 1048576 | tf_op jit(solution)/shard_map/all_to_all | solution.py:191
  110.4 8.8 %all-to-all-done.4 = bf16[128,8,256]{2,1,0:T(8,128)(2,1)S(1)} async-done(((bf16[128,8,256]{2,1,0:T(8,128)(2,1)}), bf16[128,8,256]{2,1,0:T(8,128)(2,1)S(1)}, u32[]{:S(2)}, u32[]{:S(2)}) %all-to-all-start.4) | async-done | bytes 524320 | tf_op jit(solution)/shard_map/all_to_all | solution.py:191
  119.2 0.4 copy.30
  120.0 3.4 %fusion.2 = f32[2,4,32,2048]{3,2,1,0:T(8,128)S(1)} fusion(bf16[32,2,4,1024]{3,0,2,1:T(8,128)(2,1)S(1)} %reshape.1448, bf16[1024,2048]{1,0:T(8,128)(2,1)} %pad_maximum_fusion), kind=kOutput, calls=%fused_computation.5 | convolution fusion | flops 1073741824 | bytes 6815744 | tf_op jit(solution)/shard_map/bstc,cn->stbn/dot_general | solution.py:128
  123.7 4.2 %collective-permute-start = (bf16[3,32,2048]{2,1,0:T(8,128)(2,1)S(1)}, bf16[3,32,2048]{2,1,0:T(8,128)(2,1)S(1)}, u32[]{:S(2)}, u32[]{:S(2)}) collective-permute-start(bf16[3,32,2048]{2,1,0:T(8,128)(2,1)S(1)} %slice.93), channel_id=1, source_target_pairs={{0,1},{1,2},{2,3},{4,5},{5,6},{6,7},{8,9},{9,10},{10,11},{12,13},{... | collective-permute-start | bytes 1179656 | tf_op jit(solution)/shard_map/ppermute | solution.py:20
  128.0 8.1 %collective-permute-done = bf16[3,32,2048]{2,1,0:T(8,128)(2,1)S(1)} collective-permute-done((bf16[3,32,2048]{2,1,0:T(8,128)(2,1)S(1)}, bf16[3,32,2048]{2,1,0:T(8,128)(2,1)S(1)}, u32[]{:S(2)}, u32[]{:S(2)}) %collective-permute-start) | collective-permute-done | bytes 393248 | tf_op jit(solution)/shard_map/ppermute | solution.py:20
  136.8 1.2 copy.42
  (27 shorter events, 1.8 us)
Async XLA Ops:
  7.0 6.5 %copy-start.5 = (s32[128,2]{0,1:T(2,128)S(1)}, s32[128,2]{0,1:T(2,128)}, u32[]{:S(2)}) copy-start(s32[128,2]{0,1:T(2,128)} %param.6) | copy-start | bytes 3076
  7.0 6.5 %copy-start.4 = (s32[1024,2]{0,1:T(2,128)S(1)}, s32[1024,2]{0,1:T(2,128)}, u32[]{:S(2)}) copy-start(s32[1024,2]{0,1:T(2,128)} %param.5) | copy-start | bytes 24580
  9.3 18.7 %all-to-all-start = ((bf16[4,64,8,256]{3,2,1,0:T(8,128)(2,1)}), bf16[4,64,8,256]{3,2,1,0:T(8,128)(2,1)S(1)}, u32[]{:S(2)}, u32[]{:S(2)}) async-start(bf16[4,64,8,256]{3,2,1,0:T(8,128)(2,1)} %slice_bitcast_fusion.3), calls=%async_computation | async-start | bytes 2097152 | tf_op jit(solution)/shard_map/all_to_all | solution.py:185
  30.3 20.9 %all-to-all-start.1 = ((bf16[4,64,8,256]{3,2,1,0:T(8,128)(2,1)}), bf16[4,64,8,256]{3,2,1,0:T(8,128)(2,1)}, u32[]{:S(2)}, u32[]{:S(2)}) async-start(bf16[4,64,8,256]{3,2,1,0:T(8,128)(2,1)} %slice_bitcast_fusion.2), calls=%async_computation.1 | async-start | bytes 2097152 | tf_op jit(solution)/shard_map/all_to_all | solution.py:185
  36.4 2.5 %copy-start.2 = (f32[2,1024,128]{2,1,0:T(8,128)S(1)}, f32[2,1024,128]{2,1,0:T(8,128)}, u32[]{:S(2)}) copy-start(f32[2,1024,128]{2,1,0:T(8,128)} %get-tuple-element.64.first_ref) | copy-start | bytes 3145732
  53.4 18.0 %all-to-all-start.2 = ((bf16[4,64,8,256]{3,2,1,0:T(8,128)(2,1)}), bf16[4,64,8,256]{3,2,1,0:T(8,128)(2,1)S(1)}, u32[]{:S(2)}, u32[]{:S(2)}) async-start(bf16[4,64,8,256]{3,2,1,0:T(8,128)(2,1)} %slice_bitcast_fusion.1), calls=%async_computation.2 | async-start | bytes 2097152 | tf_op jit(solution)/shard_map/all_to_all | solution.py:185
  57.0 1.2 copy-start.1
  73.7 18.8 %all-to-all-start.3 = ((bf16[4,64,8,256]{3,2,1,0:T(8,128)(2,1)}), bf16[4,64,8,256]{3,2,1,0:T(8,128)(2,1)}, u32[]{:S(2)}, u32[]{:S(2)}) async-start(bf16[4,64,8,256]{3,2,1,0:T(8,128)(2,1)} %slice_bitcast_fusion), calls=%async_computation.3 | async-start | bytes 2097152 | tf_op jit(solution)/shard_map/all_to_all | solution.py:185
  78.1 1.2 copy-start
  79.3 31.0 %copy-start.3 = (f32[4,1024]{1,0:T(4,128)S(1)}, f32[4,1024]{1,0:T(4,128)}, u32[]{:S(2)}) copy-start(f32[4,1024]{1,0:T(4,128)} %param.7) | copy-start | bytes 49156
  106.9 12.3 %all-to-all-start.4 = ((bf16[128,8,256]{2,1,0:T(8,128)(2,1)}), bf16[128,8,256]{2,1,0:T(8,128)(2,1)S(1)}, u32[]{:S(2)}, u32[]{:S(2)}) async-start(bf16[128,8,256]{2,1,0:T(8,128)(2,1)} %copy.29), calls=%async_computation.4 | async-start | bytes 1048576 | tf_op jit(solution)/shard_map/all_to_all | solution.py:191
  123.7 12.4 %collective-permute-start = (bf16[3,32,2048]{2,1,0:T(8,128)(2,1)S(1)}, bf16[3,32,2048]{2,1,0:T(8,128)(2,1)S(1)}, u32[]{:S(2)}, u32[]{:S(2)}) collective-permute-start(bf16[3,32,2048]{2,1,0:T(8,128)(2,1)S(1)} %slice.93), channel_id=1, source_target_pairs={{0,1},{1,2},{2,3},{4,5},{5,6},{6,7},{8,9},{9,10},{10,11},{12,13},{... | collective-permute-start | bytes 1179656 | tf_op jit(solution)/shard_map/ppermute | solution.py:20

commit v4 on v3

--- a/solution.py
+++ b/solution.py
@@ -10,8 +10,8 @@
 
 PHASES = 4096
 ROWS = 32
-CHUNKS = 4
-WIDTH = 8
+CHUNKS = 2
+WIDTH = 16
 
 
 def passed_along(value, axis, steps):

time: 139 us -> 129 us (0.928)
  Pallas kernels: 50.4 us -> 42.6 us
  waiting for transfers between devices: 23.6 us -> 31.2 us
  starting transfers between devices: 24.1 us -> 16.6 us
  local copies, waits for them, and re-layouts: 22.4 us -> 20.6 us
    all_to_all x4 -> x2, waiting for transfers between devices: 6.69 us -> 18.7 us  [on_device(): lax.all_to_all(turned[:, chunk], 'chan', split_axis=0, concat_axis=0, til...]
    pallas_call x4 -> x2, Pallas kernels: 50.4 us -> 42.6 us  [beamform(): pl.pallas_call(functools.partial(beam_kernel, 1.0 / math.sqrt(feeds)), gr...]
    all_to_all x4 -> x2, starting transfers between devices: 16.4 us -> 8.84 us  [on_device(): lax.all_to_all(turned[:, chunk], 'chan', split_axis=0, concat_axis=0, til...]
    all_to_all x1, waiting for transfers between devices: 8.78 us -> 4.44 us  [on_device(): lax.all_to_all(beamed, 'chan', split_axis=0, concat_axis=2, tiled=True)]
    squeeze x4 -> x2, local copies, waits for them, and re-layouts: 9.21 us -> 6.16 us  [on_device(): turned[:, chunk]]
    concatenate x1 -> x0, other arithmetic: 2.46 us -> none  [make_basis(): return jnp.concatenate([cosine, sine], axis=1)]
    convert_element_type x1, other arithmetic: 1.38 us -> 3.75 us  [make_basis(): cosine = cosine.reshape(size, size).astype(jnp.bfloat16)]
    unnamed x13 -> x17, local copies, waits for them, and re-layouts: 2.45 us -> 3.66 us
  transfers between devices with their start and end apart: 6 -> 4, of which waited for: 5 -> 4; matrix products, arithmetic and copies ran while one was open for 10% -> 11% of each run, Pallas kernels for 27% -> 16%
where the time goes in v4:
time: 129 us; the launch traced here: 128 us
  Pallas kernels  42.6 us (33%)
  waiting for transfers between devices  31.2 us (24%)
  local copies, waits for them, and re-layouts  20.6 us (16%)
  starting transfers between devices  16.6 us (13%)
  other arithmetic  14.2 us (11%)
  matrix products  2.84 us (2%)
    pallas_call x2, Pallas kernels, beamform(): pl.pallas_call(functools.partial(beam_kernel, 1.0 / math.sqrt(feeds)), gr...  42.6 us
    all_to_all x2, waiting for transfers between devices, on_device(): lax.all_to_all(turned[:, chunk], 'chan', split_axis=0, concat_axis=0, til...  18.7 us
    all_to_all x2, starting transfers between devices, on_device(): lax.all_to_all(turned[:, chunk], 'chan', split_axis=0, concat_axis=0, til...  8.84 us
    ppermute x1, waiting for transfers between devices, passed_along(): lax.ppermute(value, axis, [(source, source + steps) for source in range(i...  8.1 us
    reshape x1, local copies, waits for them, and re-layouts, on_device(): voltages.reshape(2 * frame_count, feeds, size)  6.95 us
    squeeze x2, local copies, waits for them, and re-layouts, on_device(): turned[:, chunk]  6.16 us
    sub x1, other arithmetic, times(): return (ar * br - ai * bi, ar * bi + ai * br)  5.06 us
    all_to_all x1, waiting for transfers between devices, on_device(): lax.all_to_all(beamed, 'chan', split_axis=0, concat_axis=2, tiled=True)  4.44 us
  transfers between devices with their start and end apart: 4, of which 4 were waited for; matrix products, arithmetic and copies ran while one was open for 11% of the time, Pallas kernels for 16%

profile of v4, /device:TPU:0, one launch (start us, length us, event | category | flops | bytes accessed | tf_op | source)
XLA Modules:
  0.0 128.2 jit_solution(13933255609054989578)
XLA Ops:
  0.0 7.0 %copy.27 = bf16[8,256,1024]{1,0,2:T(8,128)(2,1)} copy(bf16[8,256,1024]{2,1,0:T(8,128)(2,1)} %bitcast.48) | data formatting | bytes 8388608 | tf_op jit(solution)/shard_map/reshape | solution.py:159
  7.0 3.1 %slice_bitcast_fusion.1 = bf16[4,128,8,256]{3,2,1,0:T(8,128)(2,1)} fusion(bf16[4,2,128,8,256]{4,3,2,1,0:T(8,128)(2,1)} %bitcast.46), kind=kLoop, calls=%fused_computation.8 | loop fusion | bytes 4194304 | tf_op jit(solution)/shard_map/squeeze | solution.py:185
  10.1 4.2 %all-to-all-start = ((bf16[4,128,8,256]{3,2,1,0:T(8,128)(2,1)}), bf16[4,128,8,256]{3,2,1,0:T(8,128)(2,1)S(1)}, u32[]{:S(2)}, u32[]{:S(2)}) async-start(bf16[4,128,8,256]{3,2,1,0:T(8,128)(2,1)} %slice_bitcast_fusion.1), calls=%async_computation | async-start | bytes 4194304 | tf_op jit(solution)/shard_map/all_to_all | solution.py:185
  14.3 5.1 %multiply_subtract_fusion = (f32[1,1024,128]{2,1,0:T(8,128)S(1)}, f32[1,1024,128]{2,1,0:T(8,128)S(1)}, f32[1,1024,128]{2,1,0:T(8,128)S(1)}, f32[1,1024,128]{2,1,...) fusion(s32[128]{0:T(128)S(1)} %get-tuple-element.32, s32[1024]{0:T(1024)S(1)} %bitcast.57, ...), kind=kLoop, calls=%fused_computation.53 | loop fusion | flops 10747904 | bytes 3154948 | tf_op jit(solution)/shard_map/sub | solution.py:35
  19.4 1.0 pad_maximum_fusion.2.first_ref
  20.4 1.2 pad_maximum_fusion
  21.6 18.4 %all-to-all-done.v_ref = bf16[4,128,8,256]{3,2,1,0:T(8,128)(2,1)S(1)} async-done(((bf16[4,128,8,256]{3,2,1,0:T(8,128)(2,1)}), bf16[4,128,8,256]{3,2,1,0:T(8,128)(2,1)S(1)}, u32[]{:S(2)}, u32[]{:S(2)}) %all-to-all-start) | async-done | bytes 2097184 | tf_op jit(solution)/shard_map/all_to_all | solution.py:185
  40.0 3.1 %slice_bitcast_fusion = bf16[4,128,8,256]{3,2,1,0:T(8,128)(2,1)} fusion(bf16[4,2,128,8,256]{4,3,2,1,0:T(8,128)(2,1)} %bitcast.47), kind=kLoop, calls=%fused_computation.7 | loop fusion | bytes 4194304 | tf_op jit(solution)/shard_map/squeeze | solution.py:185
  43.0 4.6 %all-to-all-start.1 = ((bf16[4,128,8,256]{3,2,1,0:T(8,128)(2,1)}), bf16[4,128,8,256]{3,2,1,0:T(8,128)(2,1)}, u32[]{:S(2)}, u32[]{:S(2)}) async-start(bf16[4,128,8,256]{3,2,1,0:T(8,128)(2,1)} %slice_bitcast_fusion), calls=%async_computation.1 | async-start | bytes 4194304 | tf_op jit(solution)/shard_map/all_to_all | solution.py:185
  47.7 0.6 constant_dynamic-update-slice_fusion.1
  48.3 1.2 fusion.34
  49.5 1.3 %fusion.37 = (f32[32,1024]{1,0:T(8,128)}, f32[32,1024]{1,0:T(8,128)}) fusion(s32[32]{0:T(128)S(1)} %iota_multiply_fusion), kind=kLoop, calls=%fused_computation.86 | loop fusion | flops 458752 | bytes 262272 | tf_op jit(solution)/shard_map/cos | solution.py:31
  50.8 1.2 copy-done.1
  52.0 20.9 %shard_map.46 = bf16[128,8,128]{2,1,0:T(8,128)(2,1)S(1)} custom-call(bf16[4,128,8,256]{3,2,1,0:T(8,128)(2,1)S(1)} %all-to-all-done.v_ref, f32[2,1024,128]{2,1,0:T(8,128)S(1)} %copy-done.1, f32[2,1024,128]{2,1,0:T(8,128)S(1)} %get-tuple-element.12.unit_ref), custom_call_target="tpu_custom_call" | custom-call | flops 1073741824 | bytes 4194304 | tf_op jit(solution)/shard_map/pallas_call | solution.py:94
  72.9 0.3 all-to-all-done.1.v_ref
  73.2 1.2 copy-done
  74.5 21.7 %shard_map.47 = bf16[128,8,128]{2,1,0:T(8,128)(2,1)S(1)} custom-call(bf16[4,128,8,256]{3,2,1,0:T(8,128)(2,1)} %all-to-all-done.1.v_ref, f32[2,1024,128]{2,1,0:T(8,128)S(1)} %copy-done, f32[2,1024,128]{2,1,0:T(8,128)S(1)} %get-tuple-element.12.unit_ref), custom_call_target="tpu_custom_call" | custom-call | flops 1073741824 | bytes 4194304 | tf_op jit(solution)/shard_map/pallas_call | solution.py:94
  96.2 1.4 %copy.23 = bf16[128,8,256]{2,1,0:T(8,128)(2,1)} copy(bf16[128,8,256]{0,1,2:T(8,128)(2,1)S(1)} %maximum_bitcast_fusion.4) | data formatting | bytes 1048576 | tf_op jit(solution)/shard_map/transpose | solution.py:190
  97.6 3.5 %all-to-all-start.2 = ((bf16[128,8,256]{2,1,0:T(8,128)(2,1)}), bf16[128,8,256]{2,1,0:T(8,128)(2,1)S(1)}, u32[]{:S(2)}, u32[]{:S(2)}) async-start(bf16[128,8,256]{2,1,0:T(8,128)(2,1)} %copy.23), calls=%async_computation.2 | async-start | bytes 1048576 | tf_op jit(solution)/shard_map/all_to_all | solution.py:191
  101.1 0.6 copy-done.3
  101.7 3.7 %subtract_convert_fusion = (bf16[32,32,1024]{2,1,0:T(8,128)(2,1)S(1)}, bf16[32,32,1024]{2,1,0:T(8,128)(2,1)}) fusion(f32[32,1024]{1,0:T(8,128)S(1)} %get-tuple-element.37, f32[32,1024]{1,0:T(8,128)} %get-tuple-element.34, f32[32,1024]{1,0:T(8,128)} %get-tuple-element.38, f32[32,1024]{1,0:T(8,128)} %get-tuple-element.33), kind=kLoop, calls=%fused_computation.5 | loop fusion | flops 8388608 | bytes 4718592 | tf_op jit(solution)/shard_map/convert_element_type | solution.py:121
  105.4 4.4 %all-to-all-done.2 = bf16[128,8,256]{2,1,0:T(8,128)(2,1)S(1)} async-done(((bf16[128,8,256]{2,1,0:T(8,128)(2,1)}), bf16[128,8,256]{2,1,0:T(8,128)(2,1)S(1)}, u32[]{:S(2)}, u32[]{:S(2)}) %all-to-all-start.2) | async-done | bytes 524320 | tf_op jit(solution)/shard_map/all_to_all | solution.py:191
  109.9 0.4 copy.24
  110.3 0.4 reshape.1011
  110.6 2.8 %fusion.3 = f32[2,4,32,2048]{3,2,1,0:T(8,128)S(1)} fusion(bf16[32,2,4,1024]{3,0,2,1:T(8,128)(2,1)S(1)} %reshape.1011, bf16[1024,1024]{1,0:T(8,128)(2,1)} %bitcast.50, bf16[1024,1024]{1,0:T(8,128)(2,1)S(1)} %bitcast.49), kind=kOutput, calls=%fused_computation.6 | convolution fusion | flops 1082130432 | bytes 6815744 | tf_op jit(solution)/shard_map/bstc,cn->stbn/dot_general | solution.py:128
  113.5 0.2 fusion.17
  113.8 4.3 %collective-permute-start = (bf16[3,32,2048]{2,1,0:T(8,128)(2,1)S(1)}, bf16[3,32,2048]{2,1,0:T(8,128)(2,1)S(1)}, u32[]{:S(2)}, u32[]{:S(2)}) collective-permute-start(bf16[3,32,2048]{2,1,0:T(8,128)(2,1)S(1)} %slice.83), channel_id=1, source_target_pairs={{0,1},{1,2},{2,3},{4,5},{5,6},{6,7},{8,9},{9,10},{10,11},{12,13},{... | collective-permute-start | bytes 1179656 | tf_op jit(solution)/shard_map/ppermute | solution.py:20
  118.2 8.1 %collective-permute-done = bf16[3,32,2048]{2,1,0:T(8,128)(2,1)S(1)} collective-permute-done((bf16[3,32,2048]{2,1,0:T(8,128)(2,1)S(1)}, bf16[3,32,2048]{2,1,0:T(8,128)(2,1)S(1)}, u32[]{:S(2)}, u32[]{:S(2)}) %collective-permute-start) | collective-permute-done | bytes 393248 | tf_op jit(solution)/shard_map/ppermute | solution.py:20
  126.2 0.1 maximum_convert_fusion
  126.4 0.3 fusion.5
  126.6 0.4 reshape.1012
  127.0 1.2 copy.32
  (21 shorter events, 0.2 us)
Async XLA Ops:
  7.0 7.3 %copy-start.7 = (s32[128,2]{0,1:T(2,128)S(1)}, s32[128,2]{0,1:T(2,128)}, u32[]{:S(2)}) copy-start(s32[128,2]{0,1:T(2,128)} %param.6) | copy-start | bytes 3076
  7.0 7.3 %copy-start.6 = (s32[1024,2]{0,1:T(2,128)S(1)}, s32[1024,2]{0,1:T(2,128)}, u32[]{:S(2)}) copy-start(s32[1024,2]{0,1:T(2,128)} %param.5) | copy-start | bytes 24580
  10.1 29.9 %all-to-all-start = ((bf16[4,128,8,256]{3,2,1,0:T(8,128)(2,1)}), bf16[4,128,8,256]{3,2,1,0:T(8,128)(2,1)S(1)}, u32[]{:S(2)}, u32[]{:S(2)}) async-start(bf16[4,128,8,256]{3,2,1,0:T(8,128)(2,1)} %slice_bitcast_fusion.1), calls=%async_computation | async-start | bytes 4194304 | tf_op jit(solution)/shard_map/all_to_all | solution.py:185
  21.6 26.1 %copy-start.5 = (f32[4,1024]{1,0:T(4,128)S(1)}, f32[4,1024]{1,0:T(4,128)}, u32[]{:S(2)}) copy-start(f32[4,1024]{1,0:T(4,128)} %param.7) | copy-start | bytes 49156
  43.0 30.2 %all-to-all-start.1 = ((bf16[4,128,8,256]{3,2,1,0:T(8,128)(2,1)}), bf16[4,128,8,256]{3,2,1,0:T(8,128)(2,1)}, u32[]{:S(2)}, u32[]{:S(2)}) async-start(bf16[4,128,8,256]{3,2,1,0:T(8,128)(2,1)} %slice_bitcast_fusion), calls=%async_computation.1 | async-start | bytes 4194304 | tf_op jit(solution)/shard_map/all_to_all | solution.py:185
  50.8 1.2 copy-start.1
  73.2 1.2 copy-start
  74.5 26.6 %copy-start.2 = (f32[4,2048]{1,0:T(4,128)S(1)}, f32[4,2048]{1,0:T(4,128)}, u32[]{:S(2)}) copy-start(f32[4,2048]{1,0:T(4,128)} %constant_dynamic-update-slice_fusion.1) | copy-start | bytes 98308
  97.6 12.3 %all-to-all-start.2 = ((bf16[128,8,256]{2,1,0:T(8,128)(2,1)}), bf16[128,8,256]{2,1,0:T(8,128)(2,1)S(1)}, u32[]{:S(2)}, u32[]{:S(2)}) async-start(bf16[128,8,256]{2,1,0:T(8,128)(2,1)} %copy.23), calls=%async_computation.2 | async-start | bytes 1048576 | tf_op jit(solution)/shard_map/all_to_all | solution.py:191
  101.1 0.6 copy-start.3
  113.5 4.6 %copy-start.4 = (f32[4,2048]{1,0:T(4,128)S(1)}, f32[4,2048]{1,0:T(4,128)}, u32[]{:S(2)}) copy-start(f32[4,2048]{1,0:T(4,128)} %copy-done.3) | copy-start | bytes 98308
  113.8 12.5 %collective-permute-start = (bf16[3,32,2048]{2,1,0:T(8,128)(2,1)S(1)}, bf16[3,32,2048]{2,1,0:T(8,128)(2,1)S(1)}, u32[]{:S(2)}, u32[]{:S(2)}) collective-permute-start(bf16[3,32,2048]{2,1,0:T(8,128)(2,1)S(1)} %slice.83), channel_id=1, source_target_pairs={{0,1},{1,2},{2,3},{4,5},{5,6},{6,7},{8,9},{9,10},{10,11},{12,13},{... | collective-permute-start | bytes 1179656 | tf_op jit(solution)/shard_map/ppermute | solution.py:20

commit v5 on v4

--- a/solution.py
+++ b/solution.py
@@ -173,16 +173,15 @@
     blocks = []
     for chunk in range(chunks):
         if chunk == 1:
-            turned, unit, firsts = lax.optimization_barrier((turned, unit, firsts))
-        if chunk == 2:
-            turned, basis = lax.optimization_barrier((turned, basis))
+            turned, unit, firsts, basis = lax.optimization_barrier((turned, unit, firsts, basis))
         if chunk > 1:
             turned, blocks[chunk - 2] = lax.optimization_barrier((turned, blocks[chunk - 2]))
+        piece = turned[:, chunk]
         if chunk > 0:
             received, start = blocks[chunk - 1]
-            turned, received = lax.optimization_barrier((turned, received))
+            piece, received = lax.optimization_barrier((piece, received))
             blocks[chunk - 1] = (received, start)
-        received = lax.all_to_all(turned[:, chunk], "chan", split_axis=0, concat_axis=0, tiled=True)
+        received = lax.all_to_all(piece, "chan", split_axis=0, concat_axis=0, tiled=True)
         blocks.append((received, firsts[chunk]))
         if chunk > 0:
             blocks[chunk - 1] = beamform(*blocks[chunk - 1], unit)

time: 129 us -> 126 us (0.977)
  local copies, waits for them, and re-layouts: 20.6 us -> 19 us
    all_to_all x2, waiting for transfers between devices: 18.7 us -> 14.1 us  [on_device(): lax.all_to_all(piece, 'chan', split_axis=0, concat_axis=0, tiled=True)]
    all_to_all x1, waiting for transfers between devices: 4.44 us -> 8.78 us  [on_device(): lax.all_to_all(beamed, 'chan', split_axis=0, concat_axis=2, tiled=True)]
    concatenate x0 -> x1, other arithmetic: none -> 2.58 us  [make_basis(): return jnp.concatenate([cosine, sine], axis=1)]
    convert_element_type x1, other arithmetic: 3.75 us -> 1.38 us  [make_basis(): cosine = cosine.reshape(size, size).astype(jnp.bfloat16)]
    squeeze x2, local copies, waits for them, and re-layouts: 6.16 us -> 4.65 us  [on_device(): piece = turned[:, chunk]]
    unnamed x17 -> x13, local copies, waits for them, and re-layouts: 3.66 us -> 3.58 us
  transfers between devices with their start and end apart: 4 -> 4, of which waited for: 4 -> 4; matrix products, arithmetic and copies ran while one was open for 11% -> 11% of each run, Pallas kernels for 16% -> 17%
where the time goes in v5:
time: 126 us
  Pallas kernels  42.6 us (34%)
  waiting for transfers between devices  30.9 us (25%)
  local copies, waits for them, and re-layouts  19 us (15%)
  starting transfers between devices  16.6 us (13%)
  other arithmetic  13 us (10%)
  matrix products  3.44 us (3%)
    pallas_call x2, Pallas kernels, beamform(): pl.pallas_call(functools.partial(beam_kernel, 1.0 / math.sqrt(feeds)), gr...  42.6 us
    all_to_all x2, waiting for transfers between devices, on_device(): lax.all_to_all(piece, 'chan', split_axis=0, concat_axis=0, tiled=True)  14.1 us
    all_to_all x2, starting transfers between devices, on_device(): lax.all_to_all(piece, 'chan', split_axis=0, concat_axis=0, tiled=True)  8.84 us
    all_to_all x1, waiting for transfers between devices, on_device(): lax.all_to_all(beamed, 'chan', split_axis=0, concat_axis=2, tiled=True)  8.78 us
    ppermute x1, waiting for transfers between devices, passed_along(): lax.ppermute(value, axis, [(source, source + steps) for source in range(i...  8.09 us
    reshape x1, local copies, waits for them, and re-layouts, on_device(): voltages.reshape(2 * frame_count, feeds, size)  6.98 us
    sub x1, other arithmetic, times(): return (ar * br - ai * bi, ar * bi + ai * br)  5.07 us
    squeeze x2, local copies, waits for them, and re-layouts, on_device(): piece = turned[:, chunk]  4.65 us
  transfers between devices with their start and end apart: 4, of which 4 were waited for; matrix products, arithmetic and copies ran while one was open for 11% of the time, Pallas kernels for 17%

profile of v5, /device:TPU:0, one launch (start us, length us, event | category | flops | bytes accessed | tf_op | source)
XLA Modules:
  0.0 125.8 jit_solution(11787585496330873088)
XLA Ops:
  0.0 7.0 %copy.27 = bf16[8,256,1024]{1,0,2:T(8,128)(2,1)} copy(bf16[8,256,1024]{2,1,0:T(8,128)(2,1)} %bitcast.50) | data formatting | bytes 8388608 | tf_op jit(solution)/shard_map/reshape | solution.py:159
  7.0 3.1 %slice_bitcast_fusion = bf16[4,128,8,256]{3,2,1,0:T(8,128)(2,1)} fusion(bf16[4,2,128,8,256]{4,3,2,1,0:T(8,128)(2,1)} %bitcast.46), kind=kLoop, calls=%fused_computation.6 | loop fusion | bytes 4194304 | tf_op jit(solution)/shard_map/squeeze | solution.py:179
  10.1 4.2 %all-to-all-start = ((bf16[4,128,8,256]{3,2,1,0:T(8,128)(2,1)}), bf16[4,128,8,256]{3,2,1,0:T(8,128)(2,1)S(1)}, u32[]{:S(2)}, u32[]{:S(2)}) async-start(bf16[4,128,8,256]{3,2,1,0:T(8,128)(2,1)} %slice_bitcast_fusion), calls=%async_computation | async-start | bytes 4194304 | tf_op jit(solution)/shard_map/all_to_all | solution.py:184
  14.3 0.5 fusion.35
  14.9 5.1 %multiply_subtract_fusion = (f32[1,1024,128]{2,1,0:T(8,128)S(1)}, f32[1,1024,128]{2,1,0:T(8,128)S(1)}, f32[1,1024,128]{2,1,0:T(8,128)S(1)}, f32[1,1024,128]{2,1,...) fusion(s32[128]{0:T(128)S(1)} %get-tuple-element.34, s32[1024]{0:T(1024)S(1)} %bitcast.57, ...), kind=kLoop, calls=%fused_computation.52 | loop fusion | flops 10747904 | bytes 3154948 | tf_op jit(solution)/shard_map/sub | solution.py:35
  20.0 1.0 pad_maximum_fusion.3.first_ref
  21.0 1.1 pad_maximum_fusion.1
  22.2 0.6 fusion.38
  22.8 1.4 %subtract_convert_fusion = (bf16[32,32,1024]{2,1,0:T(8,128)(2,1)S(1)}, bf16[32,32,1024]{2,1,0:T(8,128)(2,1)S(1)}) fusion(f32[32,1024]{1,0:T(8,128)S(1)} %get-tuple-element.39, f32[32,1024]{1,0:T(8,128)S(1)} %get-tuple-element.36, f32[32,1024]{1,0:T(8,128)S(1)} %get-tuple-element.40, f32[32,1024]{1,0:T(8,128)S(1)} %get-tuple-element.35), kind=kLoop, calls=%fused_computation.4 | loop fusion | flops 8388608 | bytes 4718592 | tf_op jit(solution)/shard_map/convert_element_type | solution.py:121
  24.2 2.6 %pad_maximum_fusion = bf16[1024,2048]{1,0:T(8,128)(2,1)} fusion(bf16[1024,1024]{1,0:T(8,128)(2,1)S(1)} %bitcast.49, bf16[1024,1024]{1,0:T(8,128)(2,1)S(1)} %bitcast.48), kind=kLoop, calls=%fused_computation | loop fusion | flops 8388608 | bytes 8388608 | tf_op jit(solution)/shard_map/concatenate | solution.py:123
  26.7 1.1 copy-done.2
  27.9 1.5 %slice_bitcast_fusion.1 = bf16[4,128,8,256]{3,2,1,0:T(8,128)(2,1)} fusion(bf16[4,2,128,8,256]{4,3,2,1,0:T(8,128)(2,1)S(1)} %bitcast.47), kind=kLoop, calls=%fused_computation.7 | loop fusion | bytes 4194304 | tf_op jit(solution)/shard_map/squeeze | solution.py:179
  29.4 10.7 %all-to-all-done.v_ref = bf16[4,128,8,256]{3,2,1,0:T(8,128)(2,1)S(1)} async-done(((bf16[4,128,8,256]{3,2,1,0:T(8,128)(2,1)}), bf16[4,128,8,256]{3,2,1,0:T(8,128)(2,1)S(1)}, u32[]{:S(2)}, u32[]{:S(2)}) %all-to-all-start) | async-done | bytes 2097184 | tf_op jit(solution)/shard_map/all_to_all | solution.py:184
  40.0 4.6 %all-to-all-start.1 = ((bf16[4,128,8,256]{3,2,1,0:T(8,128)(2,1)}), bf16[4,128,8,256]{3,2,1,0:T(8,128)(2,1)}, u32[]{:S(2)}, u32[]{:S(2)}) async-start(bf16[4,128,8,256]{3,2,1,0:T(8,128)(2,1)} %slice_bitcast_fusion.1), calls=%async_computation.1 | async-start | bytes 4194304 | tf_op jit(solution)/shard_map/all_to_all | solution.py:184
  44.7 1.2 copy-done.1
  45.9 20.9 %shard_map.46 = bf16[128,8,128]{2,1,0:T(8,128)(2,1)S(1)} custom-call(bf16[4,128,8,256]{3,2,1,0:T(8,128)(2,1)S(1)} %all-to-all-done.v_ref, f32[2,1024,128]{2,1,0:T(8,128)S(1)} %copy-done.1, f32[2,1024,128]{2,1,0:T(8,128)S(1)} %get-tuple-element.14.unit_ref), custom_call_target="tpu_custom_call" | custom-call | flops 1073741824 | bytes 4194304 | tf_op jit(solution)/shard_map/pallas_call | solution.py:94
  66.9 3.4 %all-to-all-done.1.v_ref = bf16[4,128,8,256]{3,2,1,0:T(8,128)(2,1)} async-done(((bf16[4,128,8,256]{3,2,1,0:T(8,128)(2,1)}), bf16[4,128,8,256]{3,2,1,0:T(8,128)(2,1)}, u32[]{:S(2)}, u32[]{:S(2)}) %all-to-all-start.1) | async-done | bytes 2097184 | tf_op jit(solution)/shard_map/all_to_all | solution.py:184
  70.3 1.2 copy-done
  71.5 21.7 %shard_map.47 = bf16[128,8,128]{2,1,0:T(8,128)(2,1)S(1)} custom-call(bf16[4,128,8,256]{3,2,1,0:T(8,128)(2,1)} %all-to-all-done.1.v_ref, f32[2,1024,128]{2,1,0:T(8,128)S(1)} %copy-done, f32[2,1024,128]{2,1,0:T(8,128)S(1)} %get-tuple-element.14.unit_ref), custom_call_target="tpu_custom_call" | custom-call | flops 1073741824 | bytes 4194304 | tf_op jit(solution)/shard_map/pallas_call | solution.py:94
  93.2 1.4 %copy.23 = bf16[128,8,256]{2,1,0:T(8,128)(2,1)} copy(bf16[128,8,256]{0,1,2:T(8,128)(2,1)S(1)} %maximum_bitcast_fusion) | data formatting | bytes 1048576 | tf_op jit(solution)/shard_map/transpose | solution.py:189
  94.6 3.5 %all-to-all-start.2 = ((bf16[128,8,256]{2,1,0:T(8,128)(2,1)}), bf16[128,8,256]{2,1,0:T(8,128)(2,1)S(1)}, u32[]{:S(2)}, u32[]{:S(2)}) async-start(bf16[128,8,256]{2,1,0:T(8,128)(2,1)} %copy.23), calls=%async_computation.2 | async-start | bytes 1048576 | tf_op jit(solution)/shard_map/all_to_all | solution.py:190
  98.1 8.8 %all-to-all-done.2 = bf16[128,8,256]{2,1,0:T(8,128)(2,1)S(1)} async-done(((bf16[128,8,256]{2,1,0:T(8,128)(2,1)}), bf16[128,8,256]{2,1,0:T(8,128)(2,1)S(1)}, u32[]{:S(2)}, u32[]{:S(2)}) %all-to-all-start.2) | async-done | bytes 524320 | tf_op jit(solution)/shard_map/all_to_all | solution.py:190
  106.9 0.4 copy.24
  107.3 0.4 reshape.1011
  107.7 3.4 %fusion.2 = f32[2,4,32,2048]{3,2,1,0:T(8,128)S(1)} fusion(bf16[32,2,4,1024]{3,0,2,1:T(8,128)(2,1)S(1)} %reshape.1011, bf16[1024,2048]{1,0:T(8,128)(2,1)} %pad_maximum_fusion), kind=kOutput, calls=%fused_computation.5 | convolution fusion | flops 1073741824 | bytes 6815744 | tf_op jit(solution)/shard_map/bstc,cn->stbn/dot_general | solution.py:128
  111.1 0.1 fusion.18
  111.4 4.3 %collective-permute-start = (bf16[3,32,2048]{2,1,0:T(8,128)(2,1)S(1)}, bf16[3,32,2048]{2,1,0:T(8,128)(2,1)S(1)}, u32[]{:S(2)}, u32[]{:S(2)}) collective-permute-start(bf16[3,32,2048]{2,1,0:T(8,128)(2,1)S(1)} %slice.83), channel_id=1, source_target_pairs={{0,1},{1,2},{2,3},{4,5},{5,6},{6,7},{8,9},{9,10},{10,11},{12,13},{... | collective-permute-start | bytes 1179656 | tf_op jit(solution)/shard_map/ppermute | solution.py:20
  115.7 8.1 %collective-permute-done = bf16[3,32,2048]{2,1,0:T(8,128)(2,1)S(1)} collective-permute-done((bf16[3,32,2048]{2,1,0:T(8,128)(2,1)S(1)}, bf16[3,32,2048]{2,1,0:T(8,128)(2,1)S(1)}, u32[]{:S(2)}, u32[]{:S(2)}) %collective-permute-start) | collective-permute-done | bytes 393248 | tf_op jit(solution)/shard_map/ppermute | solution.py:20
  123.8 0.1 maximum_convert_fusion
  123.9 0.3 fusion.6
  124.2 0.4 reshape.1012
  124.6 1.2 copy.32
  (18 shorter events, 0.2 us)
Async XLA Ops:
  7.0 7.9 %copy-start.4 = (s32[1024,2]{0,1:T(2,128)S(1)}, s32[1024,2]{0,1:T(2,128)}, u32[]{:S(2)}) copy-start(s32[1024,2]{0,1:T(2,128)} %param.5) | copy-start | bytes 24580
  7.0 7.9 %copy-start.5 = (s32[128,2]{0,1:T(2,128)S(1)}, s32[128,2]{0,1:T(2,128)}, u32[]{:S(2)}) copy-start(s32[128,2]{0,1:T(2,128)} %param.6) | copy-start | bytes 3076
  10.1 29.9 %all-to-all-start = ((bf16[4,128,8,256]{3,2,1,0:T(8,128)(2,1)}), bf16[4,128,8,256]{3,2,1,0:T(8,128)(2,1)S(1)}, u32[]{:S(2)}, u32[]{:S(2)}) async-start(bf16[4,128,8,256]{3,2,1,0:T(8,128)(2,1)} %slice_bitcast_fusion), calls=%async_computation | async-start | bytes 4194304 | tf_op jit(solution)/shard_map/all_to_all | solution.py:184
  24.2 3.7 %copy-start.2 = (bf16[8,256,1024]{1,0,2:T(8,128)(2,1)S(1)}, bf16[8,256,1024]{1,0,2:T(8,128)(2,1)}, u32[]{:S(2)}) copy-start(bf16[8,256,1024]{1,0,2:T(8,128)(2,1)} %copy.27) | copy-start | bytes 12582916
  40.0 30.2 %all-to-all-start.1 = ((bf16[4,128,8,256]{3,2,1,0:T(8,128)(2,1)}), bf16[4,128,8,256]{3,2,1,0:T(8,128)(2,1)}, u32[]{:S(2)}, u32[]{:S(2)}) async-start(bf16[4,128,8,256]{3,2,1,0:T(8,128)(2,1)} %slice_bitcast_fusion.1), calls=%async_computation.1 | async-start | bytes 4194304 | tf_op jit(solution)/shard_map/all_to_all | solution.py:184
  44.7 1.2 copy-start.1
  70.3 1.2 copy-start
  71.5 26.6 %copy-start.3 = (f32[4,1024]{1,0:T(4,128)S(1)}, f32[4,1024]{1,0:T(4,128)}, u32[]{:S(2)}) copy-start(f32[4,1024]{1,0:T(4,128)} %param.7) | copy-start | bytes 49156
  94.6 12.3 %all-to-all-start.2 = ((bf16[128,8,256]{2,1,0:T(8,128)(2,1)}), bf16[128,8,256]{2,1,0:T(8,128)(2,1)S(1)}, u32[]{:S(2)}, u32[]{:S(2)}) async-start(bf16[128,8,256]{2,1,0:T(8,128)(2,1)} %copy.23), calls=%async_computation.2 | async-start | bytes 1048576 | tf_op jit(solution)/shard_map/all_to_all | solution.py:190
  111.4 12.5 %collective-permute-start = (bf16[3,32,2048]{2,1,0:T(8,128)(2,1)S(1)}, bf16[3,32,2048]{2,1,0:T(8,128)(2,1)S(1)}, u32[]{:S(2)}, u32[]{:S(2)}) collective-permute-start(bf16[3,32,2048]{2,1,0:T(8,128)(2,1)S(1)} %slice.83), channel_id=1, source_target_pairs={{0,1},{1,2},{2,3},{4,5},{5,6},{6,7},{8,9},{9,10},{10,11},{12,13},{... | collective-permute-start | bytes 1179656 | tf_op jit(solution)/shard_map/ppermute | solution.py:20
